TPU v7x, 128 devices: a whole 4x4x4 slice. The times are simulated.
128 devices in a mesh: left: 8 (over z, core), right: 16 (over x, y).
Axes of the slice: x: 4, y: 4, z: 4, core: 2. Of those that a mesh axis runs over, the one named last changes fastest.
Arguments:
- psi: bfloat16 [32, 512, 32, 512], P('left', None, 'right'), may hold values from -6 to 6
- env_left: bfloat16 [2, 32, 512, 512], P(None, 'left'), may hold values from -0.25 to 0.25
- env_right: bfloat16 [2, 32, 512, 512], P(None, 'right'), may hold values from -0.25 to 0.25
- left_target: int32 [2, 32], replicated, may hold values from 0 to 31, each once within a row
- right_target: int32 [2, 32], replicated, may hold values from 0 to 31, each once within a row
- qn_left: int32 [32], replicated, may hold values from 0 to 3
- qn_right: int32 [32], replicated, may hold values from 0 to 3
Outputs:
- sigma: bfloat16 [32, 512, 32, 512], P(None, ('left', 'right'))
Inputs may be any that keep to these rules, and one draw needn't show every extreme that they name: `left_target`: each row names every left sector exactly once. `right_target`: each row names every right sector exactly once.
All inputs are finite; a program needn't handle non-finite values.
Results may differ from a plain program's by a relative error of at most 0.0058.
Values may be sent and summed in bfloat16 or wider, within the bound.
A program may use at most 128 MiB of HBM per device.

v0:
```python
import jax
import jax.numpy as jnp
from jax import lax
from jax.sharding import PartitionSpec as P

filling_charge = 3


def local_terms(psi, env_left, env_right):
    half = jnp.einsum("taxy,aybz->taxbz", env_left, psi, preferred_element_type=jnp.float32).astype(
        jnp.bfloat16
    )
    return jnp.einsum(
        "taxbz,tbwz->tabxw", half, env_right, preferred_element_type=jnp.float32
    ).astype(jnp.bfloat16)


def source_index(left_row, right_row, left_dev, right_dev):
    n_right = lax.axis_size("right")
    inverse_left = jnp.argsort(left_row)
    inverse_right = jnp.argsort(right_row)
    source_left = inverse_left[:, None]
    source_right = inverse_right[None, :]
    owner_left = source_left // left_dev
    inner_left = source_left % left_dev
    owner_right = source_right // right_dev
    inner_right = source_right % right_dev
    flat = ((owner_left * n_right + owner_right) * left_dev + inner_left) * right_dev + inner_right
    return flat.reshape(-1)


def route(blocks):
    count, left_dev, right_dev, width, inner = blocks.shape
    flat = blocks.reshape(count, left_dev * right_dev, width, inner)
    arrived = lax.all_to_all(flat, ("left", "right"), split_axis=2, concat_axis=1, tiled=True)
    return arrived


def placed_sum(total, arrived, left_target, right_target, first, left_dev, right_dev):
    for index in range(arrived.shape[0]):
        flat = source_index(
            left_target[first + index], right_target[first + index], left_dev, right_dev
        )
        total = total + jnp.take(arrived[index], flat, axis=0).astype(jnp.float32)
    return total


def local(psi, env_left, env_right, left_target, right_target, qn_left, qn_right):
    left_dev = psi.shape[0]
    right_dev = psi.shape[2]
    sectors_left = left_target.shape[1]
    sectors_right = right_target.shape[1]
    width = psi.shape[1] // (lax.axis_size("left") * lax.axis_size("right"))
    inner = psi.shape[3]
    total = jnp.zeros((sectors_left * sectors_right, width, inner), jnp.float32)
    arrived = route(local_terms(psi, env_left, env_right))
    total = placed_sum(total, arrived, left_target, right_target, 0, left_dev, right_dev)
    total = total.reshape(sectors_left, sectors_right, width, inner)
    allowed = qn_left[:, None] + qn_right[None, :] == filling_charge
    masked = jnp.where(allowed[:, :, None, None], total, 0.0)
    return jnp.transpose(masked, (0, 2, 1, 3)).astype(jnp.bfloat16)


def solution(mesh):
    placed = (
        P("left", None, "right", None),
        P(None, "left", None, None),
        P(None, "right", None, None),
        P(),
        P(),
        P(),
        P(),
    )
    return jax.shard_map(
        local,
        mesh=mesh,
        in_specs=placed,
        out_specs=P(None, ("left", "right"), None, None),
        check_vma=False,
    )
```

profile of v0, /device:TPU:0, one launch (start us, length us, event | category | flops | bytes accessed | tf_op | source)
XLA Modules:
  0.0 213.2 jit_solution(4224861310678696114)
XLA Ops:
  0.0 0.0 copy-start
  0.0 11.3 %copy.27 = bf16[4,512,2,512]{1,3,0,2:T(8,128)(2,1)} copy(bf16[4,512,2,512]{3,2,1,0:T(2,128)(2,1)} %param.9) | data formatting | bytes 8388608 | tf_op args[0]
  11.3 0.0 copy-done
  11.3 13.3 %convert_bitcast_fusion = bf16[2,4,2,512,512]{4,3,1,2,0:T(8,128)(2,1)} fusion(bf16[2,4,512,512]{3,2,1,0:T(8,128)(2,1)} %param.10, bf16[4,512,2,512]{1,3,0,2:T(8,128)(2,1)} %copy.27, bf16[2,2,512,512]{3,2,1,0:T(8,128)(2,1)S(1)} %copy-done), kind=kOutput, calls=%fused_computation.6 | convolution fusion | flops 8598323200 | bytes 18874368 | tf_op jit(solution)/shard_map/taxbz,tbwz->tabxw/dot_general | solution.py:13
  24.6 7.3 %copy.29 = bf16[2,4,2,512,512]{4,3,2,1,0:T(8,128)(2,1)} copy(bf16[2,4,2,512,512]{4,3,1,2,0:T(8,128)(2,1)} %convert_bitcast_fusion) | data formatting | bytes 16777216 | tf_op jit(solution)/shard_map/convert_element_type | solution.py:15
  31.9 11.3 %copy.30 = bf16[2,8,512,512]{3,1,0,2:T(8,128)(2,1)} copy(bf16[2,8,512,512]{3,2,1,0:T(8,128)(2,1)} %bitcast.42) | data formatting | bytes 16777216 | tf_op jit(solution)/shard_map/reshape | solution.py:34
  43.2 0.0 copy-start.2
  43.2 0.0 copy-start.3
  43.2 0.0 copy-start.4
  43.2 0.0 copy-start.5
  43.3 11.9 %all-to-all-start = ((bf16[2,8,512,512]{3,1,0,2:T(8,128)(2,1)}), bf16[2,8,512,512]{3,1,0,2:T(8,128)(2,1)}, u32[]{:S(2)}, u32[]{:S(2)}) async-start(bf16[2,8,512,512]{3,1,0,2:T(8,128)(2,1)} %copy.30), calls=%async_computation | async-start | bytes 16777216 | tf_op jit(solution)/shard_map/all_to_all | solution.py:35
  55.1 0.0 copy-done.2
  55.2 1.6 sort.62
  56.8 0.0 copy-done.3
  56.8 1.6 sort.61
  58.4 0.1 multiply_add_fusion
  58.5 0.1 reshape.174
  58.5 1.6 sort.60
  60.2 1.6 sort.59
  61.8 0.1 multiply_add_fusion.1
  61.9 0.1 reshape.173
  62.0 0.0 copy-done.4
  62.0 0.0 copy-done.5
  62.0 0.1 add_compare_fusion
  62.1 92.0 %all-to-all-done = bf16[2,8,512,512]{3,1,0,2:T(8,128)(2,1)} async-done(((bf16[2,8,512,512]{3,1,0,2:T(8,128)(2,1)}), bf16[2,8,512,512]{3,1,0,2:T(8,128)(2,1)}, u32[]{:S(2)}, u32[]{:S(2)}) %all-to-all-start) | async-done | bytes 8388640 | tf_op jit(solution)/shard_map/all_to_all | solution.py:35
  154.1 7.3 %copy.31 = bf16[2,8,512,512]{3,1,2,0:T(8,128)(2,1)} copy(bf16[2,8,512,512]{3,1,0,2:T(8,128)(2,1)} %all-to-all-done) | data formatting | bytes 16777216 | tf_op jit(solution)/shard_map/all_to_all | solution.py:35
  161.4 3.8 %fusion.17 = (bf16[1,128,8,4,512]{4,2,3,1,0:T(8,128)(2,1)S(1)}, bf16[1,128,8,4,512]{4,2,3,1,0:T(8,128)(2,1)S(1)}) fusion(bf16[2,128,8,4,512]{4,2,3,1,0:T(8,128)(2,1)} %bitcast.41), kind=kLoop, calls=%fused_computation.50 | loop fusion | bytes 16777216 | tf_op jit(solution)/shard_map/slice | solution.py:44
  165.2 0.8 copy_bitcast_fusion
  166.0 5.3 %copy.35 = bf16[1024,4,512]{2,1,0:T(4,128)(2,1)} copy(bf16[1024,4,512]{2,0,1:T(8,128)(2,1)S(1)} %get-tuple-element.28) | data formatting | bytes 8388608 | tf_op jit(solution)/shard_map/squeeze | solution.py:44
  171.2 5.2 %copy.33 = bf16[1024,4,512]{2,1,0:T(4,128)(2,1)} copy(bf16[1024,4,512]{2,0,1:T(8,128)(2,1)S(1)} %get-tuple-element.29) | data formatting | bytes 8388608 | tf_op jit(solution)/shard_map/squeeze | solution.py:44
  176.4 13.0 %gather_fusion.1 = bf16[1024,4,512]{2,1,0:T(4,128)(2,1)} fusion(bf16[1024,4,512]{2,1,0:T(4,128)(2,1)} %copy.35, s32[1024]{0:T(1024)S(1)} %fusion.14), kind=kCustom, calls=%fused_computation.1.clone | custom fusion | bytes 8392704 | tf_op jit(solution)/shard_map/jit(_take)/gather | solution.py:44
  189.4 12.9 %gather_fusion = bf16[1024,4,512]{2,1,0:T(4,128)(2,1)} fusion(bf16[1024,4,512]{2,1,0:T(4,128)(2,1)} %copy.33, s32[1024]{0:T(1024)S(1)} %fusion.13), kind=kCustom, calls=%fused_computation.clone | custom fusion | bytes 8392704 | tf_op jit(solution)/shard_map/jit(_take)/gather | solution.py:44
  202.4 6.6 %convert_add_fusion = bf16[1024,4,512]{2,1,0:T(4,128)(2,1)S(1)} fusion(bf16[1024,4,512]{2,1,0:T(4,128)(2,1)} %gather_fusion.1, bf16[1024,4,512]{2,1,0:T(4,128)(2,1)} %gather_fusion, pred[1024]{0:T(1024)(128)(4,1)S(1)} %compare_and_fusion, pred[1024]{0:T(1024)(128)(4,1)S(1)} %compare_and_fusion.1), kind=kLoop, calls=%fused_computation.5 | loop fusion | flops 12582912 | bytes 12584960 | tf_op jit(solution)/shard_map/add | solution.py:44
  209.0 0.8 copy.36
  209.9 0.0 copy-start.1
  209.9 0.8 fusion.7
  210.6 2.5 %copy.37 = bf16[32,4,32,512]{3,2,1,0:T(8,128)(2,1)} copy(bf16[32,4,32,512]{3,2,0,1:T(8,128)(2,1)S(1)} %fusion.7) | data formatting | bytes 8388608 | tf_op jit(solution)/shard_map/convert_element_type | solution.py:61
  213.2 0.0 copy-done.1
  (12 shorter events, 0.1 us)
Async XLA Ops:
  0.0 11.3 %copy-start = (bf16[2,2,512,512]{3,2,1,0:T(8,128)(2,1)S(1)}, bf16[2,2,512,512]{3,2,1,0:T(8,128)(2,1)}, u32[]{:S(2)}) copy-start(bf16[2,2,512,512]{3,2,1,0:T(8,128)(2,1)} %param.11) | copy-start | bytes 6291460
  43.2 11.9 %copy-start.2 = (s32[2,32]{1,0:T(2,128)S(1)}, s32[2,32]{1,0:T(2,128)}, u32[]{:S(2)}) copy-start(s32[2,32]{1,0:T(2,128)} %param.13) | copy-start | bytes 772
  43.2 13.5 %copy-start.3 = (s32[2,32]{1,0:T(2,128)S(1)}, s32[2,32]{1,0:T(2,128)}, u32[]{:S(2)}) copy-start(s32[2,32]{1,0:T(2,128)} %param.12) | copy-start | bytes 772
  43.2 18.7 %copy-start.4 = (s32[32]{0:T(128)S(1)}, s32[32]{0:T(128)}, u32[]{:S(2)}) copy-start(s32[32]{0:T(128)} %param.15) | copy-start | bytes 388
  43.2 18.7 %copy-start.5 = (s32[32]{0:T(128)S(1)}, s32[32]{0:T(128)}, u32[]{:S(2)}) copy-start(s32[32]{0:T(128)} %param.14) | copy-start | bytes 388
  43.3 110.9 %all-to-all-start = ((bf16[2,8,512,512]{3,1,0,2:T(8,128)(2,1)}), bf16[2,8,512,512]{3,1,0,2:T(8,128)(2,1)}, u32[]{:S(2)}, u32[]{:S(2)}) async-start(bf16[2,8,512,512]{3,1,0,2:T(8,128)(2,1)} %copy.30), calls=%async_computation | async-start | bytes 16777216 | tf_op jit(solution)/shard_map/all_to_all | solution.py:35
  209.9 3.3 %copy-start.1 = (bf16[2,2,512,512]{3,2,1,0:T(8,128)(2,1)S(1)}, bf16[2,2,512,512]{3,2,1,0:T(8,128)(2,1)}, u32[]{:S(2)}) copy-start(bf16[2,2,512,512]{3,2,1,0:T(8,128)(2,1)} %param.11) | copy-start | bytes 6291460
where the time goes:
time: 216 us; the launch traced here: 213 us
  waiting for transfers between devices  92 us (43%)
  local copies, waits for them, and re-layouts  81.7 us (38%)
  other arithmetic  14.1 us (7%)
  matrix products  13.3 us (6%)
  starting transfers between devices  11.9 us (6%)
    all_to_all x1, waiting for transfers between devices, route(): lax.all_to_all(flat, ('left', 'right'), split_axis=2, concat_axis=1, tile...  92 us
    gather x2, local copies, waits for them, and re-layouts, placed_sum(): total = total + jnp.take(arrived[index], flat, axis=0).astype(jnp.float32)  25.9 us
    dot_general x1, matrix products, local_terms(): jnp.einsum('taxbz,tbwz->tabxw', half, env_right, preferred_element_type=j...  13.3 us
    all_to_all x1, starting transfers between devices, route(): lax.all_to_all(flat, ('left', 'right'), split_axis=2, concat_axis=1, tile...  11.9 us
    reshape x1, local copies, waits for them, and re-layouts, route(): flat = blocks.reshape(count, left_dev * right_dev, width, inner)  11.3 us
    unnamed x13, local copies, waits for them, and re-layouts  11.3 us
    squeeze x3, local copies, waits for them, and re-layouts, placed_sum(): total = total + jnp.take(arrived[index], flat, axis=0).astype(jnp.float32)  11.3 us
    convert_element_type x1, local copies, waits for them, and re-layouts, local_terms(): return jnp.einsum('taxbz,tbwz->tabxw', half, env_right, preferred_element...  7.34 us
  transfers between devices with their start and end apart: 1, of which 1 were waited for; matrix products, arithmetic and copies ran while one was open for 3% of the time, Pallas kernels for 0%

commit v1 on v0

v1 whole, which is shorter than its diff:
```python
import functools

import jax
import jax.numpy as jnp
from jax import lax
from jax.experimental import pallas as pl
from jax.experimental.pallas import tpu as pltpu
from jax.sharding import Mesh, PartitionSpec as P

filling_charge = 3
B = 512
SECTORS = 32
TERMS = 2
CHIPS_Z = 4
CORES = 2
RIGHT = 16
CHIPS = CHIPS_Z * RIGHT
LEFT_DEV = SECTORS // (CHIPS_Z * CORES)
RIGHT_DEV = SECTORS // RIGHT
ITEMS = TERMS * LEFT_DEV * RIGHT_DEV
HALF = B // CORES
ROWS = B // (CHIPS * CORES)
MESH = pl.DeviceIdType.MESH
VMEM_LIMIT = 60 * 2**20
SIZES = ((12, 12), (12, 14), (12, 16), (16, 20), (16, 32))


def table_kernel(left_target, right_target, qn_left, qn_right, items, sources, labels, most):
    f32, bf16 = jnp.float32, jnp.bfloat16
    square = (SECTORS, SECTORS)
    row = lax.broadcasted_iota(jnp.int32, square, 0)
    column = lax.broadcasted_iota(jnp.int32, square, 1)
    wide = lambda value: value.astype(f32)
    dot = lambda a, b: jnp.dot(a.astype(bf16), b.astype(bf16), preferred_element_type=f32)
    upright = lambda line: jnp.sum(
        jnp.where(row == column, wide(line), 0.0), axis=1, keepdims=True
    )
    charge_left = qn_left[...]
    charge_right = upright(qn_right[...])

    pair = wide(row // RIGHT_DEV == column // RIGHT_DEV)
    second = wide((row + 1 == column) & (column % RIGHT_DEV == 1))
    same = row // LEFT_DEV == column // LEFT_DEV
    core = wide(row // LEFT_DEV % CORES)
    swap = wide(column == row + LEFT_DEV - 2 * LEFT_DEV * (row // LEFT_DEV % CORES))
    active, to_left, to_right, rank, total = [], [], [], [], []
    for t in range(TERMS):
        lefts = upright(left_target[t : t + 1, :])
        rights = wide(right_target[t : t + 1, :])
        hit_left = wide(column) == lefts
        hit_right = wide(row) == rights
        have_left = jnp.sum(jnp.where(hit_left, wide(charge_left), 0.0), axis=1, keepdims=True)
        have_right = jnp.sum(jnp.where(hit_right, charge_right, 0.0), axis=0, keepdims=True)
        allowed = have_left + have_right == float(filling_charge)
        ones = jnp.where(allowed, 1.0, 0.0)
        count = dot(ones, pair)
        active.append(allowed)
        to_left.append(lefts)
        to_right.append(rights)
        rank.append(dot(wide(same & (column < row)), count) + dot(ones, second))
        total.append(dot(wide(same), count))
    rank[1] = rank[1] + total[0]
    own = total[0] + total[1]
    other = dot(swap, own)
    slot = [r + jnp.minimum(other, r + core) for r in rank]

    lane = lax.broadcasted_iota(jnp.int32, (SECTORS, 128), 1)
    tall = lax.broadcasted_iota(jnp.int32, (SECTORS, 128), 0)
    device_lane = tall // RIGHT_DEV == lane % RIGHT
    device_row = tall // LEFT_DEV == lane // RIGHT
    chip_row = tall // (CORES * LEFT_DEV) == lane % CHIPS // RIGHT

    def spread(steps, place, values, rows):
        stack = []
        for k in steps:
            picked = jnp.zeros(square, f32)
            for t in range(TERMS):
                picked = picked + jnp.where(
                    active[t] & (place[t] == float(k)), values[t], 0.0
                )
            stack.append(picked.astype(bf16))
        lanes = dot(jnp.concatenate(stack, axis=0), wide(device_lane))
        lanes = lanes.reshape(len(stack), SECTORS, 128)
        return jnp.sum(jnp.where(rows[None], lanes, 0.0), axis=1)

    item = wide(row % LEFT_DEV * RIGHT_DEV + column % RIGHT_DEV)
    items[...] = spread(
        range(ITEMS), rank, [item, item + float(LEFT_DEV * RIGHT_DEV)], device_row
    ).astype(jnp.int32)

    half_lane = lax.broadcasted_iota(jnp.int32, (ITEMS, 128), 1)

    def by_slot(values):
        both = spread(
            [*range(0, 2 * ITEMS, 2), *range(1, 2 * ITEMS, 2)], slot, values, chip_row
        )
        return jnp.where(half_lane < CHIPS, both[:ITEMS], both[ITEMS:])

    sources[...] = by_slot([core * ITEMS + r for r in rank]).astype(jnp.int32)
    full = jnp.zeros(square, f32)
    high = by_slot([full + lefts + 1.0 for lefts in to_left])
    low = by_slot([full + rights for rights in to_right])
    labels[...] = ((high - 1.0) * SECTORS + low).astype(jnp.int32)
    most_device = jnp.max(own)
    most_chip = jnp.max(own + other)
    choice = jnp.int32(0)
    for depth, slots in SIZES[:-1]:
        choice = choice + jnp.where(
            (most_device > float(depth)) | (most_chip > float(slots)), 1, 0
        )
    most[0, 0] = choice


def tables(left_target, right_target, qn_left, qn_right):
    vmem = pl.BlockSpec(memory_space=pltpu.VMEM)
    table = jax.ShapeDtypeStruct((ITEMS, 128), jnp.int32)
    return pl.pallas_call(
        table_kernel,
        name="tables",
        out_shape=[table, table, table, jax.ShapeDtypeStruct((1, 1), jnp.int32)],
        in_specs=[vmem] * 4,
        out_specs=[vmem] * 3 + [pl.BlockSpec(memory_space=pltpu.SMEM)],
        cost_estimate=pl.CostEstimate(flops=2**24, bytes_accessed=2**15, transcendentals=0),
    )(
        left_target,
        right_target,
        qn_left.reshape(1, SECTORS),
        qn_right.reshape(1, SECTORS),
    )


def last_count(slots):
    return 2 if slots % 4 else 4


def last_shape(count):
    return ROWS * 4 // count, count * CHIPS, B * count // 4


def onehot_rows(label, first, shape):
    row = first + lax.broadcasted_iota(jnp.int32, shape, 0)
    return jnp.where(row == label, 1.0, 0.0).astype(jnp.bfloat16)


def label_of(labels, first, count):
    return jnp.concatenate(
        [labels[pl.ds(first // 2 + p, 1), :] for p in range(count // 2)], axis=1
    )


def exchange_kernel(
    depth,
    slots,
    items,
    sources,
    labels,
    psi_hbm,
    left_hbm,
    right_hbm,
    out,
    last,
    landed,
    psi,
    left,
    right,
    product,
    both,
    send,
    arrived,
    send_pair,
    arrived_pair,
    partial,
    ordered,
    ordered_pair,
    in_sem,
    own_sem,
    pair_send_sem,
    pair_recv_sem,
    free_sem,
    self_sem,
    send_sem,
    recv_sem,
    out_sem,
):
    z = lax.axis_index("z")
    core = lax.axis_index("core")
    place = lax.axis_index("right")
    other = 1 - core
    partner = (z, other, place)
    here = z * RIGHT + place
    device = (z * CORES + core) * RIGHT + place
    fours = slots // 4
    stages = depth // 4
    ends_in_pair = slots % 4 == 2

    psi_rows = psi_hbm.reshape(LEFT_DEV, B * RIGHT_DEV, B)
    psi_load = [
        pltpu.make_async_copy(psi_rows.at[a], landed.at[a], in_sem.at[a])
        for a in range(LEFT_DEV)
    ]
    left_load = pltpu.make_async_copy(left_hbm, left, in_sem.at[LEFT_DEV])
    right_load = pltpu.make_async_copy(right_hbm, right, in_sem.at[LEFT_DEV + 1])
    for load in (*psi_load, left_load, right_load):
        load.start()

    steps = (1, 3, 2, 0)
    route = []
    for i in range(RIGHT):
        step_x = steps[i % 4]
        step_y = steps[(i + i // 4) % 4]
        far_place = (place // 4 + step_x) % 4 * 4 + (place % 4 + step_y) % 4
        route.append((step_x + step_y, steps[(i + i // 4 * 2) % 4], far_place))

    def for_others(visit):
        def turn(shift, carry):
            far_z = [(z + shift + step) % CHIPS_Z for step in range(CHIPS_Z)]
            for moved, step, far_place in route:
                if moved or step:
                    visit(far_z[step], far_place)
                else:
                    pl.when(shift > 0)(functools.partial(visit, far_z[step], far_place))
            return carry

        lax.fori_loop(0, CHIPS_Z, turn, 0)

    barrier = pltpu.get_barrier_semaphore()
    pl.semaphore_signal(barrier, inc=1, device_id=partner, device_id_type=MESH)

    def greet(far_z, far_place):
        pl.semaphore_signal(
            barrier, inc=1, device_id=(far_z, core, far_place), device_id_type=MESH
        )

    for_others(greet)

    def exchange(shape_from, shape_to):
        row = lax.broadcasted_iota(jnp.int32, (256, 256), 0)
        column = lax.broadcasted_iota(jnp.int32, (256, 256), 1)
        source = row % shape_from * shape_to + row // shape_from
        return jnp.where(column == source, 1.0, 0.0).astype(jnp.bfloat16)

    def reorder(onehot, rows):
        return jnp.dot(onehot, rows, preferred_element_type=jnp.float32).astype(
            jnp.bfloat16
        )

    unmix = exchange(128, RIGHT_DEV)

    def split(a, carry):
        pltpu.make_async_copy(psi_rows.at[a], landed.at[a], in_sem.at[a]).wait()
        for part in range(B // 128):
            apart = reorder(unmix, landed[a, part * 256 : part * 256 + 256, :])
            for b in range(RIGHT_DEV):
                psi[a * RIGHT_DEV + b, part * 128 : part * 128 + 128, :] = apart[
                    b * 128 : (b + 1) * 128
                ]
        return carry

    lax.fori_loop(0, LEFT_DEV, split, 0)
    left_load.wait()
    right_load.wait()

    def own_copy(rank):
        return pltpu.make_async_copy(
            product.at[rank, :, core], both.at[core * depth + rank], own_sem.at[rank]
        )

    def pair_copy(rank):
        return pltpu.make_async_remote_copy(
            src_ref=product.at[rank, :, other],
            dst_ref=both.at[core * depth + rank],
            send_sem=pair_send_sem.at[rank],
            recv_sem=pair_recv_sem.at[rank],
            device_id=partner,
            device_id_type=MESH,
        )

    def multiply(rank, carry):
        item = items[rank, device]
        term = item // (LEFT_DEV * RIGHT_DEV)
        pair = item % (LEFT_DEV * RIGHT_DEV)
        half = jnp.dot(
            left[term * LEFT_DEV + pair // RIGHT_DEV],
            psi[pair],
            preferred_element_type=jnp.float32,
        ).astype(jnp.bfloat16)
        moved = lax.dot_general(
            half,
            right[term * RIGHT_DEV + pair % RIGHT_DEV],
            (((1,), (1,)), ((), ())),
            preferred_element_type=jnp.float32,
        ).astype(jnp.bfloat16)
        product[rank] = moved.reshape(CHIPS_Z, CORES, B // (CHIPS_Z * CORES), B)

        @pl.when(rank == 0)
        def _():
            pl.semaphore_wait(barrier, CHIPS)

        @pl.when((rank > 0) & (rank % 4 == 0))
        def _():
            pl.semaphore_wait(free_sem, 1)

        pair_copy(rank).start()
        own_copy(rank).start()
        return carry

    def arrive(rank, carry):
        own_copy(rank).wait()
        pair_copy(rank).wait_recv()
        return carry

    def departing(outgoing, incoming, chunk, far_z, far_place):
        pltpu.make_async_remote_copy(
            src_ref=outgoing.at[far_z * RIGHT + far_place],
            dst_ref=incoming.at[here],
            send_sem=send_sem.at[chunk],
            recv_sem=recv_sem.at[chunk],
            device_id=(far_z, core, far_place),
            device_id_type=MESH,
        ).start()

    def self_copy(outgoing, incoming, chunk):
        return pltpu.make_async_copy(
            outgoing.at[here], incoming.at[here], self_sem.at[chunk]
        )

    mix = exchange(4, 64)

    def pack(outgoing, chunk, count):
        def quarter(far_z, carry):
            def block(k):
                source = sources[chunk * 2 + k // 2, k % 2 * CHIPS + here]
                return both[source // ITEMS * depth + source % ITEMS, far_z]

            blocks = [block(k) for k in range(count)]
            if count == 2:
                blocks = [rows[:, : B // 2] for rows in blocks] + [rows[:, B // 2 :] for rows in blocks]
            rows = reorder(mix, jnp.concatenate(blocks, axis=0))
            outgoing[pl.ds(far_z * RIGHT, RIGHT)] = rows.reshape(
                RIGHT, 4 * ROWS, rows.shape[-1]
            )
            return carry

        lax.fori_loop(0, CHIPS_Z, quarter, 0)

    def stage(chunk, carry):
        @pl.when(chunk < stages)
        def _():
            lax.fori_loop(4 * chunk, 4 * chunk + 4, multiply, 0)
            lax.fori_loop(4 * chunk, 4 * chunk + 4, arrive, 0)

        pack(send.at[chunk], chunk, 4)

        @pl.when(chunk < stages - 1)
        def _():
            pl.semaphore_signal(free_sem, inc=1, device_id=partner, device_id_type=MESH)

        self_copy(send.at[chunk], arrived.at[chunk], chunk).start()
        for_others(functools.partial(departing, send.at[chunk], arrived.at[chunk], chunk))
        return carry

    lax.fori_loop(0, fours, stage, 0)
    if ends_in_pair:
        pack(send_pair, fours, 2)
        self_copy(send_pair, arrived_pair, fours).start()
        for_others(functools.partial(departing, send_pair, arrived_pair, fours))

    unsort = exchange(16, 16)

    def receive(outgoing, incoming, chunk, count, sorted_rows):
        self_copy(outgoing, incoming, chunk).wait()
        arrivals = incoming.at[pl.ds(0, CHIPS - 1)]
        pltpu.make_async_copy(arrivals, arrivals, recv_sem.at[chunk]).wait()

        def sort(far_z, carry):
            rows = incoming[pl.ds(far_z * RIGHT, RIGHT)]
            rows = reorder(unsort, rows.reshape(256, rows.shape[-1]))
            for piece in range(16):
                start = pl.multiple_of(piece % count * CHIPS + far_z * RIGHT, RIGHT)
                sorted_rows[piece // count, pl.ds(start, RIGHT), :] = rows[
                    piece * RIGHT : (piece + 1) * RIGHT
                ]
            return carry

        lax.fori_loop(0, CHIPS_Z, sort, 0)

    partial[...] = jnp.zeros(partial.shape, partial.dtype)
    placed = fours if ends_in_pair else fours - 1

    def collect(chunk, carry):
        receive(send.at[chunk], arrived.at[chunk], chunk, 4, ordered)

        @pl.when(chunk < placed)
        def _():
            label = label_of(labels, chunk * 4, 4)

            def put(part, carry):
                onehot = onehot_rows(label, part * 256, (256, 4 * CHIPS))

                def row(x, carry):
                    total = jnp.dot(
                        onehot, ordered[x], preferred_element_type=jnp.float32
                    ).reshape(8, SECTORS, B)
                    total = total + partial[pl.ds(part * 8, 8), x].astype(jnp.float32)
                    partial[pl.ds(part * 8, 8), x] = total.astype(jnp.bfloat16)
                    return carry

                return lax.fori_loop(0, ROWS, row, carry, unroll=2)

            lax.fori_loop(0, SECTORS // 8, put, 0)

        @pl.when(chunk == placed - 1)
        def _():
            pltpu.make_async_copy(partial, out, out_sem.at[0]).start()

        return carry

    lax.fori_loop(0, fours, collect, 0)
    rest = ordered
    if ends_in_pair:
        receive(send_pair, arrived_pair, fours, 2, ordered_pair)
        rest = ordered_pair
    rest_out = pltpu.make_async_copy(rest, last, out_sem.at[1])
    rest_out.start()

    def sent(rank, carry):
        pair_copy(rank).wait_send()
        return carry

    lax.fori_loop(0, depth, sent, 0)

    def gone(chunk, carry):
        departures = send.at[chunk, pl.ds(0, CHIPS - 1)]
        pltpu.make_async_copy(departures, departures, send_sem.at[chunk]).wait()
        return carry

    lax.fori_loop(0, fours, gone, 0)
    if ends_in_pair:
        departures = send_pair.at[pl.ds(0, CHIPS - 1)]
        pltpu.make_async_copy(departures, departures, send_sem.at[fours]).wait()
    pltpu.make_async_copy(partial, out, out_sem.at[0]).wait()
    rest_out.wait()


def exchanged(depth, slots, items, sources, labels, psi, env_left, env_right):
    smem = pl.BlockSpec(memory_space=pltpu.SMEM)
    anywhere = pl.BlockSpec(memory_space=pl.ANY)
    vmem = pl.BlockSpec(memory_space=pltpu.VMEM)
    bf16 = jnp.bfloat16
    fours = slots // 4
    messages = (CHIPS, 4 * ROWS, B)
    pair_messages = (CHIPS, 4 * ROWS, B // 2)
    dma = pltpu.SemaphoreType.DMA
    return pl.pallas_call(
        functools.partial(exchange_kernel, depth, slots),
        name=f"exchange_{slots}",
        out_shape=[
            jax.ShapeDtypeStruct((SECTORS, ROWS, SECTORS, B), bf16),
            jax.ShapeDtypeStruct(last_shape(last_count(slots)), bf16),
        ],
        in_specs=[smem] * 2 + [vmem] + [anywhere] * 3,
        out_specs=[anywhere] * 2,
        scratch_shapes=[
            pltpu.VMEM((LEFT_DEV, B * RIGHT_DEV, B), bf16),
            pltpu.VMEM((LEFT_DEV * RIGHT_DEV, B, B), bf16),
            pltpu.VMEM((TERMS * LEFT_DEV, B, B), bf16),
            pltpu.VMEM((TERMS * RIGHT_DEV, B, B), bf16),
            pltpu.VMEM((depth, CHIPS_Z, CORES, B // (CHIPS_Z * CORES), B), bf16),
            pltpu.VMEM((CORES * depth, CHIPS_Z, B // (CHIPS_Z * CORES), B), bf16),
            pltpu.VMEM((fours, *messages), bf16),
            pltpu.VMEM((fours, *messages), bf16),
            pltpu.VMEM(pair_messages, bf16),
            pltpu.VMEM(pair_messages, bf16),
            pltpu.VMEM((SECTORS, ROWS, SECTORS, B), bf16),
            pltpu.VMEM(last_shape(4), bf16),
            pltpu.VMEM(last_shape(2), bf16),
            dma((LEFT_DEV + 2,)),
            dma((depth,)),
            dma((depth,)),
            dma((depth,)),
            pltpu.SemaphoreType.REGULAR,
            dma((fours + 1,)),
            dma((fours + 1,)),
            dma((fours + 1,)),
            dma((2,)),
        ],
        compiler_params=pltpu.CompilerParams(
            collective_id=slots // 2,
            has_side_effects=True,
            vmem_limit_bytes=VMEM_LIMIT,
        ),
        cost_estimate=pl.CostEstimate(
            flops=4 * depth * B**3, bytes_accessed=14 * 2**20, transcendentals=0
        ),
    )(
        items,
        sources,
        labels,
        psi,
        env_left.reshape(TERMS * LEFT_DEV, B, B),
        env_right.reshape(TERMS * RIGHT_DEV, B, B),
    )


def finish_kernel(first, count, labels, partial, last, out, onehot):
    @pl.when((pl.program_id(0) == 0) & (pl.program_id(1) == 0))
    def _():
        label = label_of(labels, first, count)

        def build(part, carry):
            onehot[pl.ds(pl.multiple_of(part * 256, 256), 256), :] = onehot_rows(
                label, part * 256, (256, count * CHIPS)
            )
            return carry

        lax.fori_loop(0, SECTORS * SECTORS // 256, build, 0)

    def put(part, carry):
        total = jnp.dot(
            onehot[pl.ds(pl.multiple_of(part * 256, 256), 256), :],
            last[0],
            preferred_element_type=jnp.float32,
        ).reshape(8, SECTORS, last.shape[-1])
        old = partial[pl.ds(part * 8, 8), 0].astype(jnp.float32)
        out[pl.ds(part * 8, 8), 0] = (total + old).astype(jnp.bfloat16)
        return carry

    lax.fori_loop(0, SECTORS // 8, put, 0, unroll=2)


def finished(slots, labels, partial, last):
    count = last_count(slots)
    pieces, height, width = last_shape(count)
    halves = B // width
    block = pl.BlockSpec((SECTORS, 1, SECTORS, width), lambda x, w: (0, x, 0, w))
    return pl.pallas_call(
        functools.partial(finish_kernel, slots - count, count),
        name=f"finish_{slots}",
        grid=(ROWS, halves),
        out_shape=jax.ShapeDtypeStruct((SECTORS, ROWS, SECTORS, B), jnp.bfloat16),
        in_specs=[
            pl.BlockSpec((ITEMS, 128), lambda x, w: (0, 0)),
            block,
            pl.BlockSpec((1, height, width), lambda x, w: (x * halves + w, 0, 0)),
        ],
        out_specs=block,
        scratch_shapes=[pltpu.VMEM((SECTORS * SECTORS, height), jnp.bfloat16)],
        compiler_params=pltpu.CompilerParams(vmem_limit_bytes=VMEM_LIMIT),
        cost_estimate=pl.CostEstimate(
            flops=2 * SECTORS**2 * count * CHIPS * ROWS * B,
            bytes_accessed=9 * 2**20,
            transcendentals=0,
        ),
    )(labels, partial, last)


def local(psi, env_left, env_right, left_target, right_target, qn_left, qn_right):
    items, sources, labels, choice = tables(left_target, right_target, qn_left, qn_right)

    def branch(depth, slots, operands):
        labels = operands[2]
        return finished(slots, labels, *exchanged(depth, slots, *operands))

    return lax.switch(
        choice[0, 0],
        [functools.partial(branch, depth, slots) for depth, slots in SIZES],
        (items, sources, labels, psi, env_left, env_right),
    )


def solution(mesh):
    fine = Mesh(
        mesh.devices.reshape(CHIPS_Z, CORES, RIGHT), ("z", "core", "right")
    )
    left = ("z", "core")
    return jax.shard_map(
        local,
        mesh=fine,
        in_specs=(
            P(left, None, "right", None),
            P(None, left, None, None),
            P(None, "right", None, None),
            P(),
            P(),
            P(),
            P(),
        ),
        out_specs=P(None, ("z", "core", "right"), None, None),
        check_vma=False,
    )
```

time: 216 us -> 74.1 us (0.34)
  waiting for transfers between devices: 92 us -> 0 us
  local copies, waits for them, and re-layouts: 81.7 us -> 0 us
  Pallas kernels: 0 us -> 72.1 us
  other arithmetic: 14.1 us -> 0 us
  matrix products: 13.3 us -> 0 us
  starting transfers between devices: 11.9 us -> 0 us
    all_to_all x1 -> x0, waiting for transfers between devices: 92 us -> none  [route(): lax.all_to_all(flat, ('left', 'right'), split_axis=2, concat_axis=1, tile...]
    pallas_call x0 -> x3, Pallas kernels: none -> 72.1 us  [the longest x1 61.5 us: exchanged(): pl.pallas_call(functools.partial(exchange_kernel, depth, slots), name=f'e...]
    gather x2 -> x0, local copies, waits for them, and re-layouts: 25.9 us -> none  [placed_sum(): total = total + jnp.take(arrived[index], flat, axis=0).astype(jnp.float32)]
    dot_general x1 -> x0, matrix products: 13.3 us -> none  [local_terms(): jnp.einsum('taxbz,tbwz->tabxw', half, env_right, preferred_element_type=j...]
    all_to_all x1 -> x0, starting transfers between devices: 11.9 us -> none  [route(): lax.all_to_all(flat, ('left', 'right'), split_axis=2, concat_axis=1, tile...]
    reshape x1 -> x0, local copies, waits for them, and re-layouts: 11.3 us -> none  [route(): flat = blocks.reshape(count, left_dev * right_dev, width, inner)]
    unnamed x13 -> x0, local copies, waits for them, and re-layouts: 11.3 us -> none
    squeeze x5 -> x0, local copies, waits for them, and re-layouts: 11.3 us -> none  [the longest x3 11.3 us: placed_sum(): total = total + jnp.take(arrived[index], flat, axis=0).astype(jnp.float32)]
  transfers between devices with their start and end apart: 1 -> 0, of which waited for: 1 -> 0; matrix products, arithmetic and copies ran while one was open for 3% -> 0% of each run, Pallas kernels for 0% -> 0%
where the time goes in v1:
time: 74.1 us; the launch traced here: 72.8 us
  Pallas kernels  72.1 us (97%)
    pallas_call x1, Pallas kernels, exchanged(): pl.pallas_call(functools.partial(exchange_kernel, depth, slots), name=f'e...  61.5 us
    pallas_call x1, Pallas kernels, finished(): pl.pallas_call(functools.partial(finish_kernel, slots - count, count), na...  8.18 us
    pallas_call x1, Pallas kernels, tables(): pl.pallas_call(table_kernel, name='tables', out_shape=[table, table, tabl...  2.43 us

profile of v1, /device:TPU:0, one launch (start us, length us, event | category | flops | bytes accessed | tf_op | source)
XLA Modules:
  0.0 72.8 jit_solution(1166890416570151023)
XLA Ops:
  0.0 2.4 %tables.1 = (s32[16,128]{1,0:T(8,128)S(1)}, s32[16,128]{1,0:T(8,128)S(1)}, s32[16,128]{1,0:T(8,128)S(1)}, s32[1,1]{1,0:T(1,128)}) custom-call(s32[2,32]{1,0:T(2,128)} %left_target.1, s32[2,32]{1,0:T(2,128)} %right_target.1, s32[1,32]{1,0:T(1,128)} %bitcast.23, s32[1,32]{1,0:T(1,128)} %bitcast.24), custom_call_target="tpu_custom_call" | custom-call | flops 16777216 | bytes 32768 | tf_op jit(solution)/shard_map/tables/pallas_call | solution.py:117
  3.1 69.7 %conditional.1 = (bf16[32,4,32,512]{3,2,1,0:T(8,128)(2,1)}) conditional(s32[]{:T(128)} %bitcast.12, (bf16[2,4,512,512]{3,2,1,0:T(8,128)(2,1)}, bf16[2,2,512,512]{3,2,1,0:T(8,128)(2,1)}, s32[16,128]{1,0:T(8,128)S(1)}, s32[16,128]{1,0:T(8,128)S(1)}, s32[16,128]{1,0:T(8,128)S(1)}, ...), branch_computations={%region_0.0_spmd, %region_1.0_spmd, %region_2.0_spmd, %region_3.0_... | conditional | flops 9663676416 | bytes 24117256 | solution.py:564
  3.1 61.5 %exchange_14.1 = (bf16[32,4,32,512]{3,2,1,0:T(8,128)(2,1)}, bf16[8,128,256]{2,1,0:T(8,128)(2,1)}) custom-call(s32[16,128]{1,0:T(8,128)S(1)} %get-tuple-element.80.items, s32[16,128]{1,0:T(8,128)S(1)} %get-tuple-element.81.sources, s32[16,128]{1,0:T(8,128)S(1)} %get-tuple-element.79.labels, bf16[4,512,2,512]{3,2,1,0:T(2,128)(2,1)} %get-tuple-element.82.psi_hbm, ...), custom_call_target="tpu_custom_call" | custom-call | flops 6442450944 | bytes 14680064 | tf_op jit(solution)/shard_map/cond/branch_1_fun/exchange_14/pallas_call | solution.py:454
  64.6 8.2 %finish_14.1 = bf16[32,4,32,512]{3,2,1,0:T(8,128)(2,1)} custom-call(s32[16,128]{1,0:T(8,128)S(1)} %get-tuple-element.79.labels, bf16[32,4,32,512]{3,2,1,0:T(8,128)(2,1)} %get-tuple-element.85.partial, bf16[8,128,256]{2,1,0:T(8,128)(2,1)} %get-tuple-element.86.last), custom_call_target="tpu_custom_call" | custom-call | flops 536870912 | bytes 9437184 | tf_op jit(solution)/shard_map/cond/branch_1_fun/finish_14/pallas_call | solution.py:536

commit v2 on v1

--- a/solution.py
+++ b/solution.py
@@ -22,7 +22,7 @@
 ROWS = B // (CHIPS * CORES)
 MESH = pl.DeviceIdType.MESH
 VMEM_LIMIT = 60 * 2**20
-SIZES = ((12, 12), (12, 14), (12, 16), (16, 20), (16, 32))
+SIZES = ((10, 12), (10, 14), (12, 16), (12, 18), (16, 32))
 
 
 def table_kernel(left_target, right_target, qn_left, qn_right, items, sources, labels, most):
@@ -190,7 +190,7 @@
     here = z * RIGHT + place
     device = (z * CORES + core) * RIGHT + place
     fours = slots // 4
-    stages = depth // 4
+    stages = -(-depth // 4)
     ends_in_pair = slots % 4 == 2
 
     psi_rows = psi_hbm.reshape(LEFT_DEV, B * RIGHT_DEV, B)
@@ -200,7 +200,7 @@
     ]
     left_load = pltpu.make_async_copy(left_hbm, left, in_sem.at[LEFT_DEV])
     right_load = pltpu.make_async_copy(right_hbm, right, in_sem.at[LEFT_DEV + 1])
-    for load in (*psi_load, left_load, right_load):
+    for load in psi_load:
         load.start()
 
     steps = (1, 3, 2, 0)
@@ -211,17 +211,25 @@
         far_place = (place // 4 + step_x) % 4 * 4 + (place % 4 + step_y) % 4
         route.append((step_x + step_y, steps[(i + i // 4 * 2) % 4], far_place))
 
-    def for_others(visit):
-        def turn(shift, carry):
+    def some_others(visit, first, last):
+        def turn(shift):
             far_z = [(z + shift + step) % CHIPS_Z for step in range(CHIPS_Z)]
-            for moved, step, far_place in route:
+            for moved, step, far_place in route[first:last]:
                 if moved or step:
                     visit(far_z[step], far_place)
                 else:
                     pl.when(shift > 0)(functools.partial(visit, far_z[step], far_place))
+
+        return turn
+
+    def for_others(visit, first=0, last=RIGHT):
+        turn = some_others(visit, first, last)
+
+        def turned(shift, carry):
+            turn(shift)
             return carry
 
-        lax.fori_loop(0, CHIPS_Z, turn, 0)
+        lax.fori_loop(0, CHIPS_Z, turned, 0)
 
     barrier = pltpu.get_barrier_semaphore()
     pl.semaphore_signal(barrier, inc=1, device_id=partner, device_id_type=MESH)
@@ -247,7 +255,6 @@
     unmix = exchange(128, RIGHT_DEV)
 
     def split(a, carry):
-        pltpu.make_async_copy(psi_rows.at[a], landed.at[a], in_sem.at[a]).wait()
         for part in range(B // 128):
             apart = reorder(unmix, landed[a, part * 256 : part * 256 + 256, :])
             for b in range(RIGHT_DEV):
@@ -256,7 +263,16 @@
                 ]
         return carry
 
-    lax.fori_loop(0, LEFT_DEV, split, 0)
+    psi_load[0].wait()
+    left_load.start()
+    right_load.start()
+    split(0, 0)
+
+    def next_split(a, carry):
+        pltpu.make_async_copy(psi_rows.at[a], landed.at[a], in_sem.at[a]).wait()
+        return split(a, carry)
+
+    lax.fori_loop(1, LEFT_DEV, next_split, 0)
     left_load.wait()
     right_load.wait()
 
@@ -275,7 +291,7 @@
             device_id_type=MESH,
         )
 
-    def multiply(rank, carry):
+    def multiply(rank):
         item = items[rank, device]
         term = item // (LEFT_DEV * RIGHT_DEV)
         pair = item % (LEFT_DEV * RIGHT_DEV)
@@ -292,17 +308,9 @@
         ).astype(jnp.bfloat16)
         product[rank] = moved.reshape(CHIPS_Z, CORES, B // (CHIPS_Z * CORES), B)
 
-        @pl.when(rank == 0)
-        def _():
-            pl.semaphore_wait(barrier, CHIPS)
-
-        @pl.when((rank > 0) & (rank % 4 == 0))
-        def _():
-            pl.semaphore_wait(free_sem, 1)
-
+    def swap(rank):
         pair_copy(rank).start()
         own_copy(rank).start()
-        return carry
 
     def arrive(rank, carry):
         own_copy(rank).wait()
@@ -341,14 +349,13 @@
             )
             return carry
 
-        lax.fori_loop(0, CHIPS_Z, quarter, 0)
-
-    def stage(chunk, carry):
-        @pl.when(chunk < stages)
-        def _():
-            lax.fori_loop(4 * chunk, 4 * chunk + 4, multiply, 0)
-            lax.fori_loop(4 * chunk, 4 * chunk + 4, arrive, 0)
-
+        lax.fori_loop(0, CHIPS_Z, quarter, 0, unroll=2)
+
+    def leave(chunk):
+        return functools.partial(departing, send.at[chunk], arrived.at[chunk], chunk)
+
+    def packed(chunk, ready):
+        lax.fori_loop(4 * chunk, ready, arrive, 0)
         pack(send.at[chunk], chunk, 4)
 
         @pl.when(chunk < stages - 1)
@@ -356,10 +363,46 @@
             pl.semaphore_signal(free_sem, inc=1, device_id=partner, device_id_type=MESH)
 
         self_copy(send.at[chunk], arrived.at[chunk], chunk).start()
-        for_others(functools.partial(departing, send.at[chunk], arrived.at[chunk], chunk))
-        return carry
-
-    lax.fori_loop(0, fours, stage, 0)
+
+    def first(rank, carry):
+        multiply(rank)
+
+        @pl.when(rank == 0)
+        def _():
+            pl.semaphore_wait(barrier, CHIPS)
+
+        swap(rank)
+        return carry
+
+    lax.fori_loop(0, 4, first, 0)
+    packed(0, 4)
+
+    def stage(chunk, carry):
+        for_others(leave(chunk - 1), 0, 4)
+        turn = some_others(leave(chunk - 1), 4, RIGHT)
+        count = jnp.clip(depth - 4 * chunk, 0, 4)
+
+        @pl.when(chunk < stages)
+        def _():
+            pl.semaphore_wait(free_sem, 1)
+
+        def both_at_once(step, carry):
+            turn(step)
+            multiply(4 * chunk + step)
+            swap(4 * chunk + step)
+            return carry
+
+        def send_only(step, carry):
+            turn(step)
+            return carry
+
+        lax.fori_loop(0, count, both_at_once, 0)
+        lax.fori_loop(count, CHIPS_Z, send_only, 0)
+        packed(chunk, 4 * chunk + count)
+        return carry
+
+    lax.fori_loop(1, fours, stage, 0)
+    for_others(leave(fours - 1))
     if ends_in_pair:
         pack(send_pair, fours, 2)
         self_copy(send_pair, arrived_pair, fours).start()
@@ -502,49 +545,59 @@
     )
 
 
-def finish_kernel(first, count, labels, partial, last, out, onehot):
-    @pl.when((pl.program_id(0) == 0) & (pl.program_id(1) == 0))
-    def _():
-        label = label_of(labels, first, count)
-
-        def build(part, carry):
-            onehot[pl.ds(pl.multiple_of(part * 256, 256), 256), :] = onehot_rows(
-                label, part * 256, (256, count * CHIPS)
-            )
-            return carry
-
-        lax.fori_loop(0, SECTORS * SECTORS // 256, build, 0)
-
-    def put(part, carry):
-        total = jnp.dot(
-            onehot[pl.ds(pl.multiple_of(part * 256, 256), 256), :],
-            last[0],
-            preferred_element_type=jnp.float32,
-        ).reshape(8, SECTORS, last.shape[-1])
-        old = partial[pl.ds(part * 8, 8), 0].astype(jnp.float32)
-        out[pl.ds(part * 8, 8), 0] = (total + old).astype(jnp.bfloat16)
-        return carry
-
-    lax.fori_loop(0, SECTORS // 8, put, 0, unroll=2)
+def finish_kernel(first, count, labels, partial, last, out, held, rest, sem, rest_sem):
+    parts = held.shape[0] // 8
+
+    def fetch(part):
+        rows = pl.ds(part * 8, 8)
+        return pltpu.make_async_copy(partial.at[rows], held.at[rows], sem.at[part])
+
+    def store(part):
+        rows = pl.ds(part * 8, 8)
+        return pltpu.make_async_copy(held.at[rows], out.at[rows], sem.at[part])
+
+    rest_fetch = pltpu.make_async_copy(last, rest, rest_sem)
+    rest_fetch.start()
+    for part in range(parts):
+        fetch(part).start()
+    label = label_of(labels, first, count)
+    rest_fetch.wait()
+
+    def add(part, carry):
+        onehot = onehot_rows(label, part * 256, (256, count * CHIPS))
+        fetch(part).wait()
+        width = rest.shape[-1]
+        for piece in range(rest.shape[0]):
+            x, lanes = piece * width // B, piece * width % B
+            lanes = slice(lanes, lanes + width)
+            total = jnp.dot(
+                onehot, rest[piece], preferred_element_type=jnp.float32
+            ).reshape(8, SECTORS, width)
+            total = total + held[pl.ds(part * 8, 8), x, :, lanes].astype(jnp.float32)
+            held[pl.ds(part * 8, 8), x, :, lanes] = total.astype(jnp.bfloat16)
+        store(part).start()
+        return carry
+
+    lax.fori_loop(0, parts, add, 0)
+    for part in range(parts):
+        store(part).wait()
 
 
 def finished(slots, labels, partial, last):
     count = last_count(slots)
-    pieces, height, width = last_shape(count)
-    halves = B // width
-    block = pl.BlockSpec((SECTORS, 1, SECTORS, width), lambda x, w: (0, x, 0, w))
+    anywhere = pl.BlockSpec(memory_space=pl.ANY)
     return pl.pallas_call(
         functools.partial(finish_kernel, slots - count, count),
         name=f"finish_{slots}",
-        grid=(ROWS, halves),
-        out_shape=jax.ShapeDtypeStruct((SECTORS, ROWS, SECTORS, B), jnp.bfloat16),
-        in_specs=[
-            pl.BlockSpec((ITEMS, 128), lambda x, w: (0, 0)),
-            block,
-            pl.BlockSpec((1, height, width), lambda x, w: (x * halves + w, 0, 0)),
+        out_shape=jax.ShapeDtypeStruct(partial.shape, partial.dtype),
+        in_specs=[pl.BlockSpec(memory_space=pltpu.VMEM), anywhere, anywhere],
+        out_specs=anywhere,
+        scratch_shapes=[
+            pltpu.VMEM(partial.shape, partial.dtype),
+            pltpu.VMEM(last.shape, last.dtype),
+            pltpu.SemaphoreType.DMA((SECTORS // 8,)),
+            pltpu.SemaphoreType.DMA,
         ],
-        out_specs=block,
-        scratch_shapes=[pltpu.VMEM((SECTORS * SECTORS, height), jnp.bfloat16)],
         compiler_params=pltpu.CompilerParams(vmem_limit_bytes=VMEM_LIMIT),
         cost_estimate=pl.CostEstimate(
             flops=2 * SECTORS**2 * count * CHIPS * ROWS * B,

time: 74.1 us -> 71.8 us (0.969)
  Pallas kernels: 72.1 us -> 69.6 us
    pallas_call x1, Pallas kernels: 8.18 us -> 4.75 us  [finished(): pl.pallas_call(functools.partial(finish_kernel, slots - count, count), na...]
    pallas_call x1, Pallas kernels: 61.5 us -> 62.4 us  [exchanged(): pl.pallas_call(functools.partial(exchange_kernel, depth, slots), name=f'e...]
where the time goes in v2:
time: 71.8 us; the launch traced here: 70.7 us
  Pallas kernels  69.6 us (97%)
  between operations  0.84 us (1%)
    pallas_call x1, Pallas kernels, exchanged(): pl.pallas_call(functools.partial(exchange_kernel, depth, slots), name=f'e...  62.4 us
    pallas_call x1, Pallas kernels, finished(): pl.pallas_call(functools.partial(finish_kernel, slots - count, count), na...  4.75 us
    pallas_call x1, Pallas kernels, tables(): pl.pallas_call(table_kernel, name='tables', out_shape=[table, table, tabl...  2.43 us

profile of v2, /device:TPU:0, one launch (start us, length us, event | category | flops | bytes accessed | tf_op | source)
XLA Modules:
  0.0 70.7 jit_solution(30999503547587814)
XLA Ops:
  0.0 2.4 %tables.1 = (s32[16,128]{1,0:T(8,128)S(1)}, s32[16,128]{1,0:T(8,128)S(1)}, s32[16,128]{1,0:T(8,128)S(1)}, s32[1,1]{1,0:T(1,128)}) custom-call(s32[2,32]{1,0:T(2,128)} %left_target.1, s32[2,32]{1,0:T(2,128)} %right_target.1, s32[1,32]{1,0:T(1,128)} %bitcast.23, s32[1,32]{1,0:T(1,128)} %bitcast.24), custom_call_target="tpu_custom_call" | custom-call | flops 16777216 | bytes 32768 | tf_op jit(solution)/shard_map/tables/pallas_call | solution.py:117
  3.1 67.4 %conditional.1 = (bf16[32,4,32,512]{3,2,1,0:T(8,128)(2,1)}) conditional(s32[]{:T(128)} %bitcast.12, (bf16[2,4,512,512]{3,2,1,0:T(8,128)(2,1)}, bf16[2,2,512,512]{3,2,1,0:T(8,128)(2,1)}, s32[16,128]{1,0:T(8,128)S(1)}, s32[16,128]{1,0:T(8,128)S(1)}, s32[16,128]{1,0:T(8,128)S(1)}, ...), branch_computations={%region_0.0_spmd, %region_1.0_spmd, %region_2.0_spmd, %region_3.0_... | conditional | flops 9663676416 | bytes 24117256 | solution.py:617
  3.1 62.4 %exchange_14.1 = (bf16[32,4,32,512]{3,2,1,0:T(8,128)(2,1)}, bf16[8,128,256]{2,1,0:T(8,128)(2,1)}) custom-call(s32[16,128]{1,0:T(8,128)S(1)} %get-tuple-element.80.items, s32[16,128]{1,0:T(8,128)S(1)} %get-tuple-element.81.sources, s32[16,128]{1,0:T(8,128)S(1)} %get-tuple-element.79.labels, bf16[4,512,2,512]{3,2,1,0:T(2,128)(2,1)} %get-tuple-element.82.psi_hbm, ...), custom_call_target="tpu_custom_call" | custom-call | flops 5368709120 | bytes 14680064 | tf_op jit(solution)/shard_map/cond/branch_1_fun/exchange_14/pallas_call | solution.py:497
  65.5 4.8 %finish_14.1 = bf16[32,4,32,512]{3,2,1,0:T(8,128)(2,1)} custom-call(s32[16,128]{1,0:T(8,128)S(1)} %get-tuple-element.79.labels, bf16[32,4,32,512]{3,2,1,0:T(8,128)(2,1)} %get-tuple-element.85.partial, bf16[8,128,256]{2,1,0:T(8,128)(2,1)} %get-tuple-element.86.last), custom_call_target="tpu_custom_call" | custom-call | flops 536870912 | bytes 9437184 | tf_op jit(solution)/shard_map/cond/branch_1_fun/finish_14/pallas_call | solution.py:589

commit v3 on v2

--- a/solution.py
+++ b/solution.py
@@ -129,8 +129,12 @@
     )
 
 
+def fours_of(slots):
+    return (slots - 2) // 4
+
+
 def last_count(slots):
-    return 2 if slots % 4 else 4
+    return 4 if slots % 4 == 2 else 2
 
 
 def last_shape(count):
@@ -189,9 +193,9 @@
     partner = (z, other, place)
     here = z * RIGHT + place
     device = (z * CORES + core) * RIGHT + place
-    fours = slots // 4
-    stages = -(-depth // 4)
-    ends_in_pair = slots % 4 == 2
+    fours = fours_of(slots)
+    stages = -(-(depth + 2) // 4)
+    ends_in_pair = last_count(slots) == 2
 
     psi_rows = psi_hbm.reshape(LEFT_DEV, B * RIGHT_DEV, B)
     psi_load = [
@@ -204,32 +208,28 @@
         load.start()
 
     steps = (1, 3, 2, 0)
+    way = 1 - 2 * core
     route = []
     for i in range(RIGHT):
         step_x = steps[i % 4]
         step_y = steps[(i + i // 4) % 4]
-        far_place = (place // 4 + step_x) % 4 * 4 + (place % 4 + step_y) % 4
-        route.append((step_x + step_y, steps[(i + i // 4 * 2) % 4], far_place))
-
-    def some_others(visit, first, last):
-        def turn(shift):
-            far_z = [(z + shift + step) % CHIPS_Z for step in range(CHIPS_Z)]
-            for moved, step, far_place in route[first:last]:
+        far_x = (place // 4 + 4 + way * step_x) % 4
+        far_y = (place % 4 + 4 + way * step_y) % 4
+        route.append((step_x + step_y, steps[(i + i // 4 * 2) % 4], far_x * 4 + far_y))
+
+    def for_others(visit):
+        def turn(shift, carry):
+            far_z = [
+                (z + 2 * CHIPS_Z + way * (shift + step)) % CHIPS_Z for step in range(CHIPS_Z)
+            ]
+            for moved, step, far_place in route:
                 if moved or step:
                     visit(far_z[step], far_place)
                 else:
                     pl.when(shift > 0)(functools.partial(visit, far_z[step], far_place))
-
-        return turn
-
-    def for_others(visit, first=0, last=RIGHT):
-        turn = some_others(visit, first, last)
-
-        def turned(shift, carry):
-            turn(shift)
             return carry
 
-        lax.fori_loop(0, CHIPS_Z, turned, 0)
+        lax.fori_loop(0, CHIPS_Z, turn, 0)
 
     barrier = pltpu.get_barrier_semaphore()
     pl.semaphore_signal(barrier, inc=1, device_id=partner, device_id_type=MESH)
@@ -291,7 +291,7 @@
             device_id_type=MESH,
         )
 
-    def multiply(rank):
+    def multiply(rank, carry):
         item = items[rank, device]
         term = item // (LEFT_DEV * RIGHT_DEV)
         pair = item % (LEFT_DEV * RIGHT_DEV)
@@ -308,115 +308,128 @@
         ).astype(jnp.bfloat16)
         product[rank] = moved.reshape(CHIPS_Z, CORES, B // (CHIPS_Z * CORES), B)
 
-    def swap(rank):
+        @pl.when(rank == 0)
+        def _():
+            pl.semaphore_wait(barrier, CHIPS)
+
+        @pl.when((rank > 0) & (rank % 4 == 2))
+        def _():
+            pl.semaphore_wait(free_sem, 1)
+
         pair_copy(rank).start()
         own_copy(rank).start()
+        return carry
 
     def arrive(rank, carry):
         own_copy(rank).wait()
         pair_copy(rank).wait_recv()
         return carry
 
-    def departing(outgoing, incoming, chunk, far_z, far_place):
-        pltpu.make_async_remote_copy(
-            src_ref=outgoing.at[far_z * RIGHT + far_place],
-            dst_ref=incoming.at[here],
-            send_sem=send_sem.at[chunk],
-            recv_sem=recv_sem.at[chunk],
-            device_id=(far_z, core, far_place),
-            device_id_type=MESH,
+    def depart(outgoing, incoming, chunk, part=()):
+        pltpu.make_async_copy(
+            outgoing.at[here, *part], incoming.at[here, *part], self_sem.at[chunk]
         ).start()
 
-    def self_copy(outgoing, incoming, chunk):
-        return pltpu.make_async_copy(
-            outgoing.at[here], incoming.at[here], self_sem.at[chunk]
-        )
+        def start(far_z, far_place):
+            pltpu.make_async_remote_copy(
+                src_ref=outgoing.at[far_z * RIGHT + far_place, *part],
+                dst_ref=incoming.at[here, *part],
+                send_sem=send_sem.at[chunk],
+                recv_sem=recv_sem.at[chunk],
+                device_id=(far_z, core, far_place),
+                device_id_type=MESH,
+            ).start()
+
+        for_others(start)
+
+    def self_wait(outgoing, incoming, chunk, part=()):
+        pltpu.make_async_copy(
+            outgoing.at[here, *part], incoming.at[here, *part], self_sem.at[chunk]
+        ).wait()
+
+    def others_wait(buffer, sem, part=()):
+        others = buffer.at[pl.ds(0, CHIPS - 1), *part]
+        pltpu.make_async_copy(others, others, sem).wait()
+
+    def seat(four):
+        return (four + 1) // 2, (four + 1) % 2
+
+    def for_message(four, visit):
+        message, half = seat(four)
+        single = (four == 0) | ((four == fours - 1) & (half == 0))
+        pl.when(single)(lambda: visit(message, (half,)))
+        pl.when((half == 1) & (four > 0))(lambda: visit(message, ()))
+
+    def for_first(four, visit):
+        message, half = seat(four)
+        single = (four == 0) | ((four == fours - 1) & (half == 0))
+        pl.when(single)(lambda: visit(message, (half,)))
+        pl.when((half == 0) & (four < fours - 1))(lambda: visit(message, ()))
 
     mix = exchange(4, 64)
 
-    def pack(outgoing, chunk, count):
+    def pack(outgoing, first, count, part=()):
         def quarter(far_z, carry):
             def block(k):
-                source = sources[chunk * 2 + k // 2, k % 2 * CHIPS + here]
+                source = sources[first // 2 + k // 2, k % 2 * CHIPS + here]
                 return both[source // ITEMS * depth + source % ITEMS, far_z]
 
             blocks = [block(k) for k in range(count)]
             if count == 2:
                 blocks = [rows[:, : B // 2] for rows in blocks] + [rows[:, B // 2 :] for rows in blocks]
             rows = reorder(mix, jnp.concatenate(blocks, axis=0))
-            outgoing[pl.ds(far_z * RIGHT, RIGHT)] = rows.reshape(
+            outgoing[pl.ds(far_z * RIGHT, RIGHT), *part] = rows.reshape(
                 RIGHT, 4 * ROWS, rows.shape[-1]
             )
             return carry
 
         lax.fori_loop(0, CHIPS_Z, quarter, 0, unroll=2)
 
-    def leave(chunk):
-        return functools.partial(departing, send.at[chunk], arrived.at[chunk], chunk)
-
-    def packed(chunk, ready):
-        lax.fori_loop(4 * chunk, ready, arrive, 0)
-        pack(send.at[chunk], chunk, 4)
-
-        @pl.when(chunk < stages - 1)
+    messages = send.shape[0]
+
+    def stage(turn, carry):
+        start = jnp.maximum(4 * turn - 2, 0)
+        stop = jnp.maximum(jnp.minimum(4 * turn + 2, depth), start)
+        lax.fori_loop(start, stop, multiply, 0)
+        lax.fori_loop(start, stop, arrive, 0)
+
+        @pl.when(turn == 0)
+        def _():
+            pack(send_pair.at[0], 0, 2)
+            depart(send_pair.at[0], arrived_pair.at[0], messages)
+
+        @pl.when(turn > 0)
+        def _():
+            four = turn - 1
+            message, half = seat(four)
+            pack(send.at[message], 2 + 4 * four, 4, (half,))
+            for_message(
+                four,
+                lambda message, part: depart(
+                    send.at[message], arrived.at[message], message, part
+                ),
+            )
+
+        @pl.when(turn < stages - 1)
         def _():
             pl.semaphore_signal(free_sem, inc=1, device_id=partner, device_id_type=MESH)
 
-        self_copy(send.at[chunk], arrived.at[chunk], chunk).start()
-
-    def first(rank, carry):
-        multiply(rank)
-
-        @pl.when(rank == 0)
-        def _():
-            pl.semaphore_wait(barrier, CHIPS)
-
-        swap(rank)
-        return carry
-
-    lax.fori_loop(0, 4, first, 0)
-    packed(0, 4)
-
-    def stage(chunk, carry):
-        for_others(leave(chunk - 1), 0, 4)
-        turn = some_others(leave(chunk - 1), 4, RIGHT)
-        count = jnp.clip(depth - 4 * chunk, 0, 4)
-
-        @pl.when(chunk < stages)
-        def _():
-            pl.semaphore_wait(free_sem, 1)
-
-        def both_at_once(step, carry):
-            turn(step)
-            multiply(4 * chunk + step)
-            swap(4 * chunk + step)
-            return carry
-
-        def send_only(step, carry):
-            turn(step)
-            return carry
-
-        lax.fori_loop(0, count, both_at_once, 0)
-        lax.fori_loop(count, CHIPS_Z, send_only, 0)
-        packed(chunk, 4 * chunk + count)
-        return carry
-
-    lax.fori_loop(1, fours, stage, 0)
-    for_others(leave(fours - 1))
+        return carry
+
+    lax.fori_loop(0, fours + 1, stage, 0)
     if ends_in_pair:
-        pack(send_pair, fours, 2)
-        self_copy(send_pair, arrived_pair, fours).start()
-        for_others(functools.partial(departing, send_pair, arrived_pair, fours))
+        pack(send_pair.at[1], slots - 2, 2)
+        depart(send_pair.at[1], arrived_pair.at[1], messages + 1)
 
     unsort = exchange(16, 16)
 
-    def receive(outgoing, incoming, chunk, count, sorted_rows):
-        self_copy(outgoing, incoming, chunk).wait()
-        arrivals = incoming.at[pl.ds(0, CHIPS - 1)]
-        pltpu.make_async_copy(arrivals, arrivals, recv_sem.at[chunk]).wait()
-
+    def receive(outgoing, incoming, chunk, part=()):
+        self_wait(outgoing, incoming, chunk, part)
+        others_wait(incoming, recv_sem.at[chunk], part)
+
+    def ordering(incoming, count, sorted_rows, part=()):
         def sort(far_z, carry):
-            rows = incoming[pl.ds(far_z * RIGHT, RIGHT)]
+            rows = incoming[pl.ds(far_z * RIGHT, RIGHT), *part]
             rows = reorder(unsort, rows.reshape(256, rows.shape[-1]))
             for piece in range(16):
                 start = pl.multiple_of(piece % count * CHIPS + far_z * RIGHT, RIGHT)
@@ -428,31 +441,50 @@
         lax.fori_loop(0, CHIPS_Z, sort, 0)
 
     partial[...] = jnp.zeros(partial.shape, partial.dtype)
+
+    def place_chunk(first, count, sorted_rows):
+        label = label_of(labels, first, count)
+        pieces, _, width = sorted_rows.shape
+
+        def put(part, carry):
+            onehot = onehot_rows(label, part * 256, (256, count * CHIPS))
+
+            def row(x, carry):
+                for half in range(pieces // ROWS):
+                    lanes = slice(half * width, half * width + width)
+                    total = jnp.dot(
+                        onehot,
+                        sorted_rows[x * (pieces // ROWS) + half],
+                        preferred_element_type=jnp.float32,
+                    ).reshape(8, SECTORS, width)
+                    total = total + partial[pl.ds(part * 8, 8), x, :, lanes].astype(jnp.float32)
+                    partial[pl.ds(part * 8, 8), x, :, lanes] = total.astype(jnp.bfloat16)
+                return carry
+
+            return lax.fori_loop(0, ROWS, row, carry, unroll=2)
+
+        lax.fori_loop(0, SECTORS // 8, put, 0)
+
+    receive(send_pair.at[0], arrived_pair.at[0], messages)
+    ordering(arrived_pair.at[0], 2, ordered_pair)
+    place_chunk(0, 2, ordered_pair)
     placed = fours if ends_in_pair else fours - 1
 
-    def collect(chunk, carry):
-        receive(send.at[chunk], arrived.at[chunk], chunk, 4, ordered)
-
-        @pl.when(chunk < placed)
+    def collect(four, carry):
+        for_first(
+            four,
+            lambda message, part: receive(
+                send.at[message], arrived.at[message], message, part
+            ),
+        )
+        message, half = seat(four)
+        ordering(arrived.at[message], 4, ordered, (half,))
+
+        @pl.when(four < placed)
         def _():
-            label = label_of(labels, chunk * 4, 4)
-
-            def put(part, carry):
-                onehot = onehot_rows(label, part * 256, (256, 4 * CHIPS))
-
-                def row(x, carry):
-                    total = jnp.dot(
-                        onehot, ordered[x], preferred_element_type=jnp.float32
-                    ).reshape(8, SECTORS, B)
-                    total = total + partial[pl.ds(part * 8, 8), x].astype(jnp.float32)
-                    partial[pl.ds(part * 8, 8), x] = total.astype(jnp.bfloat16)
-                    return carry
-
-                return lax.fori_loop(0, ROWS, row, carry, unroll=2)
-
-            lax.fori_loop(0, SECTORS // 8, put, 0)
-
-        @pl.when(chunk == placed - 1)
+            place_chunk(2 + 4 * four, 4, ordered)
+
+        @pl.when(four == placed - 1)
         def _():
             pltpu.make_async_copy(partial, out, out_sem.at[0]).start()
 
@@ -461,7 +493,8 @@
     lax.fori_loop(0, fours, collect, 0)
     rest = ordered
     if ends_in_pair:
-        receive(send_pair, arrived_pair, fours, 2, ordered_pair)
+        receive(send_pair.at[1], arrived_pair.at[1], messages + 1)
+        ordering(arrived_pair.at[1], 2, ordered_pair)
         rest = ordered_pair
     rest_out = pltpu.make_async_copy(rest, last, out_sem.at[1])
     rest_out.start()
@@ -472,15 +505,16 @@
 
     lax.fori_loop(0, depth, sent, 0)
 
-    def gone(chunk, carry):
-        departures = send.at[chunk, pl.ds(0, CHIPS - 1)]
-        pltpu.make_async_copy(departures, departures, send_sem.at[chunk]).wait()
+    def gone(four, carry):
+        for_message(
+            four,
+            lambda message, part: others_wait(send.at[message], send_sem.at[message], part),
+        )
         return carry
 
     lax.fori_loop(0, fours, gone, 0)
-    if ends_in_pair:
-        departures = send_pair.at[pl.ds(0, CHIPS - 1)]
-        pltpu.make_async_copy(departures, departures, send_sem.at[fours]).wait()
+    for pair in range(1 + ends_in_pair):
+        others_wait(send_pair.at[pair], send_sem.at[messages + pair])
     pltpu.make_async_copy(partial, out, out_sem.at[0]).wait()
     rest_out.wait()
 
@@ -490,9 +524,10 @@
     anywhere = pl.BlockSpec(memory_space=pl.ANY)
     vmem = pl.BlockSpec(memory_space=pltpu.VMEM)
     bf16 = jnp.bfloat16
-    fours = slots // 4
-    messages = (CHIPS, 4 * ROWS, B)
-    pair_messages = (CHIPS, 4 * ROWS, B // 2)
+    fours = fours_of(slots)
+    messages = fours // 2 + 1
+    message = (CHIPS, 2, 4 * ROWS, B)
+    pair_messages = (2, CHIPS, 4 * ROWS, B // 2)
     dma = pltpu.SemaphoreType.DMA
     return pl.pallas_call(
         functools.partial(exchange_kernel, depth, slots),
@@ -510,8 +545,8 @@
             pltpu.VMEM((TERMS * RIGHT_DEV, B, B), bf16),
             pltpu.VMEM((depth, CHIPS_Z, CORES, B // (CHIPS_Z * CORES), B), bf16),
             pltpu.VMEM((CORES * depth, CHIPS_Z, B // (CHIPS_Z * CORES), B), bf16),
-            pltpu.VMEM((fours, *messages), bf16),
-            pltpu.VMEM((fours, *messages), bf16),
+            pltpu.VMEM((messages, *message), bf16),
+            pltpu.VMEM((messages, *message), bf16),
             pltpu.VMEM(pair_messages, bf16),
             pltpu.VMEM(pair_messages, bf16),
             pltpu.VMEM((SECTORS, ROWS, SECTORS, B), bf16),
@@ -522,9 +557,9 @@
             dma((depth,)),
             dma((depth,)),
             pltpu.SemaphoreType.REGULAR,
-            dma((fours + 1,)),
-            dma((fours + 1,)),
-            dma((fours + 1,)),
+            dma((messages + 2,)),
+            dma((messages + 2,)),
+            dma((messages + 2,)),
             dma((2,)),
         ],
         compiler_params=pltpu.CompilerParams(

time: 71.8 us -> 62.6 us (0.87); the launches traced: 70.7 us -> 62.5 us
  Pallas kernels: 69.6 us -> 61.4 us
    pallas_call x1, Pallas kernels: 62.4 us -> 54.2 us  [exchanged(): pl.pallas_call(functools.partial(exchange_kernel, depth, slots), name=f'e...]
where the time goes in v3:
time: 62.6 us; the launch traced here: 62.5 us
  Pallas kernels  61.4 us (98%)
  between operations  0.84 us (1%)
    pallas_call x1, Pallas kernels, exchanged(): pl.pallas_call(functools.partial(exchange_kernel, depth, slots), name=f'e...  54.2 us
    pallas_call x1, Pallas kernels, finished(): pl.pallas_call(functools.partial(finish_kernel, slots - count, count), na...  4.75 us
    pallas_call x1, Pallas kernels, tables(): pl.pallas_call(table_kernel, name='tables', out_shape=[table, table, tabl...  2.43 us

profile of v3, /device:TPU:0, one launch (start us, length us, event | category | flops | bytes accessed | tf_op | source)
XLA Modules:
  0.0 62.5 jit_solution(6921642294845814609)
XLA Ops:
  0.0 2.4 %tables.1 = (s32[16,128]{1,0:T(8,128)S(1)}, s32[16,128]{1,0:T(8,128)S(1)}, s32[16,128]{1,0:T(8,128)S(1)}, s32[1,1]{1,0:T(1,128)}) custom-call(s32[2,32]{1,0:T(2,128)} %left_target.1, s32[2,32]{1,0:T(2,128)} %right_target.1, s32[1,32]{1,0:T(1,128)} %bitcast.23, s32[1,32]{1,0:T(1,128)} %bitcast.24), custom_call_target="tpu_custom_call" | custom-call | flops 16777216 | bytes 32768 | tf_op jit(solution)/shard_map/tables/pallas_call | solution.py:117
  3.1 59.2 %conditional.1 = (bf16[32,4,32,512]{3,2,1,0:T(8,128)(2,1)}) conditional(s32[]{:T(128)} %bitcast.12, (bf16[2,4,512,512]{3,2,1,0:T(8,128)(2,1)}, bf16[2,2,512,512]{3,2,1,0:T(8,128)(2,1)}, s32[16,128]{1,0:T(8,128)S(1)}, s32[16,128]{1,0:T(8,128)S(1)}, s32[16,128]{1,0:T(8,128)S(1)}, ...), branch_computations={%region_0.0_spmd, %region_1.0_spmd, %region_2.0_spmd, %region_3.0_... | conditional | flops 9126805504 | bytes 24117256 | solution.py:652
  3.1 54.2 %exchange_12.1 = (bf16[32,4,32,512]{3,2,1,0:T(8,128)(2,1)}, bf16[8,128,256]{2,1,0:T(8,128)(2,1)}) custom-call(s32[16,128]{1,0:T(8,128)S(1)} %get-tuple-element.70.items, s32[16,128]{1,0:T(8,128)S(1)} %get-tuple-element.72.sources, s32[16,128]{1,0:T(8,128)S(1)} %get-tuple-element.62.labels, bf16[4,512,2,512]{3,2,1,0:T(2,128)(2,1)} %get-tuple-element.74.psi_hbm, ...), custom_call_target="tpu_custom_call" | custom-call | flops 5368709120 | bytes 14680064 | tf_op jit(solution)/shard_map/cond/branch_0_fun/exchange_12/pallas_call | solution.py:532
  57.3 4.8 %finish_12.1 = bf16[32,4,32,512]{3,2,1,0:T(8,128)(2,1)} custom-call(s32[16,128]{1,0:T(8,128)S(1)} %get-tuple-element.62.labels, bf16[32,4,32,512]{3,2,1,0:T(8,128)(2,1)} %get-tuple-element.77.partial, bf16[8,128,256]{2,1,0:T(8,128)(2,1)} %get-tuple-element.78.last), custom_call_target="tpu_custom_call" | custom-call | flops 536870912 | bytes 9437184 | tf_op jit(solution)/shard_map/cond/branch_0_fun/finish_12/pallas_call | solution.py:624

commit v4 on v3

--- a/solution.py
+++ b/solution.py
@@ -150,6 +150,33 @@
     return jnp.concatenate(
         [labels[pl.ds(first // 2 + p, 1), :] for p in range(count // 2)], axis=1
     )
+
+
+def exchange(shape_from, shape_to):
+    row = lax.broadcasted_iota(jnp.int32, (256, 256), 0)
+    column = lax.broadcasted_iota(jnp.int32, (256, 256), 1)
+    source = row % shape_from * shape_to + row // shape_from
+    return jnp.where(column == source, 1.0, 0.0).astype(jnp.bfloat16)
+
+
+def reorder(onehot, rows):
+    return jnp.dot(onehot, rows, preferred_element_type=jnp.float32).astype(jnp.bfloat16)
+
+
+def order(incoming, count, sorted_rows):
+    unsort = exchange(16, 16)
+
+    def sort(far_z, carry):
+        rows = incoming[pl.ds(far_z * RIGHT, RIGHT)]
+        rows = reorder(unsort, rows.reshape(256, rows.shape[-1]))
+        for piece in range(16):
+            start = pl.multiple_of(piece % count * CHIPS + far_z * RIGHT, RIGHT)
+            sorted_rows[piece // count, pl.ds(start, RIGHT), :] = rows[
+                piece * RIGHT : (piece + 1) * RIGHT
+            ]
+        return carry
+
+    lax.fori_loop(0, CHIPS_Z, sort, 0, unroll=2)
 
 
 def exchange_kernel(
@@ -241,17 +268,6 @@
 
     for_others(greet)
 
-    def exchange(shape_from, shape_to):
-        row = lax.broadcasted_iota(jnp.int32, (256, 256), 0)
-        column = lax.broadcasted_iota(jnp.int32, (256, 256), 1)
-        source = row % shape_from * shape_to + row // shape_from
-        return jnp.where(column == source, 1.0, 0.0).astype(jnp.bfloat16)
-
-    def reorder(onehot, rows):
-        return jnp.dot(onehot, rows, preferred_element_type=jnp.float32).astype(
-            jnp.bfloat16
-        )
-
     unmix = exchange(128, RIGHT_DEV)
 
     def split(a, carry):
@@ -291,33 +307,37 @@
             device_id_type=MESH,
         )
 
-    def multiply(rank, carry):
-        item = items[rank, device]
-        term = item // (LEFT_DEV * RIGHT_DEV)
-        pair = item % (LEFT_DEV * RIGHT_DEV)
-        half = jnp.dot(
-            left[term * LEFT_DEV + pair // RIGHT_DEV],
-            psi[pair],
-            preferred_element_type=jnp.float32,
-        ).astype(jnp.bfloat16)
-        moved = lax.dot_general(
-            half,
-            right[term * RIGHT_DEV + pair % RIGHT_DEV],
-            (((1,), (1,)), ((), ())),
-            preferred_element_type=jnp.float32,
-        ).astype(jnp.bfloat16)
-        product[rank] = moved.reshape(CHIPS_Z, CORES, B // (CHIPS_Z * CORES), B)
-
-        @pl.when(rank == 0)
+    def multiply_two(step, carry):
+        ranks = (2 * step, 2 * step + 1)
+        halves, rights = [], []
+        for rank in ranks:
+            item = items[rank, device]
+            term = item // (LEFT_DEV * RIGHT_DEV)
+            pair = item % (LEFT_DEV * RIGHT_DEV)
+            half = jnp.dot(
+                left[term * LEFT_DEV + pair // RIGHT_DEV],
+                psi[pair],
+                preferred_element_type=jnp.float32,
+            )
+            halves.append(half.astype(jnp.bfloat16))
+            rights.append(right[term * RIGHT_DEV + pair % RIGHT_DEV])
+        for rank, half, by in zip(ranks, halves, rights):
+            moved = lax.dot_general(
+                half, by, (((1,), (1,)), ((), ())), preferred_element_type=jnp.float32
+            ).astype(jnp.bfloat16)
+            product[rank] = moved.reshape(CHIPS_Z, CORES, B // (CHIPS_Z * CORES), B)
+
+        @pl.when(step == 0)
         def _():
             pl.semaphore_wait(barrier, CHIPS)
 
-        @pl.when((rank > 0) & (rank % 4 == 2))
+        @pl.when((step > 0) & (step % 2 == 1))
         def _():
             pl.semaphore_wait(free_sem, 1)
 
-        pair_copy(rank).start()
-        own_copy(rank).start()
+        for rank in ranks:
+            pair_copy(rank).start()
+            own_copy(rank).start()
         return carry
 
     def arrive(rank, carry):
@@ -325,50 +345,24 @@
         pair_copy(rank).wait_recv()
         return carry
 
-    def depart(outgoing, incoming, chunk, part=()):
-        pltpu.make_async_copy(
-            outgoing.at[here, *part], incoming.at[here, *part], self_sem.at[chunk]
+    def departing(outgoing, incoming, chunk, far_z, far_place):
+        pltpu.make_async_remote_copy(
+            src_ref=outgoing.at[far_z * RIGHT + far_place],
+            dst_ref=incoming.at[here],
+            send_sem=send_sem.at[chunk],
+            recv_sem=recv_sem.at[chunk],
+            device_id=(far_z, core, far_place),
+            device_id_type=MESH,
         ).start()
 
-        def start(far_z, far_place):
-            pltpu.make_async_remote_copy(
-                src_ref=outgoing.at[far_z * RIGHT + far_place, *part],
-                dst_ref=incoming.at[here, *part],
-                send_sem=send_sem.at[chunk],
-                recv_sem=recv_sem.at[chunk],
-                device_id=(far_z, core, far_place),
-                device_id_type=MESH,
-            ).start()
-
-        for_others(start)
-
-    def self_wait(outgoing, incoming, chunk, part=()):
-        pltpu.make_async_copy(
-            outgoing.at[here, *part], incoming.at[here, *part], self_sem.at[chunk]
-        ).wait()
-
-    def others_wait(buffer, sem, part=()):
-        others = buffer.at[pl.ds(0, CHIPS - 1), *part]
-        pltpu.make_async_copy(others, others, sem).wait()
-
-    def seat(four):
-        return (four + 1) // 2, (four + 1) % 2
-
-    def for_message(four, visit):
-        message, half = seat(four)
-        single = (four == 0) | ((four == fours - 1) & (half == 0))
-        pl.when(single)(lambda: visit(message, (half,)))
-        pl.when((half == 1) & (four > 0))(lambda: visit(message, ()))
-
-    def for_first(four, visit):
-        message, half = seat(four)
-        single = (four == 0) | ((four == fours - 1) & (half == 0))
-        pl.when(single)(lambda: visit(message, (half,)))
-        pl.when((half == 0) & (four < fours - 1))(lambda: visit(message, ()))
+    def self_copy(outgoing, incoming, chunk):
+        return pltpu.make_async_copy(
+            outgoing.at[here], incoming.at[here], self_sem.at[chunk]
+        )
 
     mix = exchange(4, 64)
 
-    def pack(outgoing, first, count, part=()):
+    def pack(outgoing, first, count):
         def quarter(far_z, carry):
             def block(k):
                 source = sources[first // 2 + k // 2, k % 2 * CHIPS + here]
@@ -378,37 +372,32 @@
             if count == 2:
                 blocks = [rows[:, : B // 2] for rows in blocks] + [rows[:, B // 2 :] for rows in blocks]
             rows = reorder(mix, jnp.concatenate(blocks, axis=0))
-            outgoing[pl.ds(far_z * RIGHT, RIGHT), *part] = rows.reshape(
+            outgoing[pl.ds(far_z * RIGHT, RIGHT)] = rows.reshape(
                 RIGHT, 4 * ROWS, rows.shape[-1]
             )
             return carry
 
         lax.fori_loop(0, CHIPS_Z, quarter, 0, unroll=2)
 
-    messages = send.shape[0]
+    def packed(outgoing, incoming, chunk, first, count):
+        pack(outgoing, first, count)
+        self_copy(outgoing, incoming, chunk).start()
+        for_others(functools.partial(departing, outgoing, incoming, chunk))
 
     def stage(turn, carry):
         start = jnp.maximum(4 * turn - 2, 0)
         stop = jnp.maximum(jnp.minimum(4 * turn + 2, depth), start)
-        lax.fori_loop(start, stop, multiply, 0)
+        lax.fori_loop(start // 2, stop // 2, multiply_two, 0)
         lax.fori_loop(start, stop, arrive, 0)
 
         @pl.when(turn == 0)
         def _():
-            pack(send_pair.at[0], 0, 2)
-            depart(send_pair.at[0], arrived_pair.at[0], messages)
+            packed(send_pair.at[0], arrived_pair.at[0], fours, 0, 2)
 
         @pl.when(turn > 0)
         def _():
             four = turn - 1
-            message, half = seat(four)
-            pack(send.at[message], 2 + 4 * four, 4, (half,))
-            for_message(
-                four,
-                lambda message, part: depart(
-                    send.at[message], arrived.at[message], message, part
-                ),
-            )
+            packed(send.at[four], arrived.at[four], four, 2 + 4 * four, 4)
 
         @pl.when(turn < stages - 1)
         def _():
@@ -418,27 +407,12 @@
 
     lax.fori_loop(0, fours + 1, stage, 0)
     if ends_in_pair:
-        pack(send_pair.at[1], slots - 2, 2)
-        depart(send_pair.at[1], arrived_pair.at[1], messages + 1)
-
-    unsort = exchange(16, 16)
-
-    def receive(outgoing, incoming, chunk, part=()):
-        self_wait(outgoing, incoming, chunk, part)
-        others_wait(incoming, recv_sem.at[chunk], part)
-
-    def ordering(incoming, count, sorted_rows, part=()):
-        def sort(far_z, carry):
-            rows = incoming[pl.ds(far_z * RIGHT, RIGHT), *part]
-            rows = reorder(unsort, rows.reshape(256, rows.shape[-1]))
-            for piece in range(16):
-                start = pl.multiple_of(piece % count * CHIPS + far_z * RIGHT, RIGHT)
-                sorted_rows[piece // count, pl.ds(start, RIGHT), :] = rows[
-                    piece * RIGHT : (piece + 1) * RIGHT
-                ]
-            return carry
-
-        lax.fori_loop(0, CHIPS_Z, sort, 0)
+        packed(send_pair.at[1], arrived_pair.at[1], fours + 1, slots - 2, 2)
+
+    def receive(outgoing, incoming, chunk):
+        self_copy(outgoing, incoming, chunk).wait()
+        arrivals = incoming.at[pl.ds(0, CHIPS - 1)]
+        pltpu.make_async_copy(arrivals, arrivals, recv_sem.at[chunk]).wait()
 
     partial[...] = jnp.zeros(partial.shape, partial.dtype)
 
@@ -465,23 +439,17 @@
 
         lax.fori_loop(0, SECTORS // 8, put, 0)
 
-    receive(send_pair.at[0], arrived_pair.at[0], messages)
-    ordering(arrived_pair.at[0], 2, ordered_pair)
+    receive(send_pair.at[0], arrived_pair.at[0], fours)
+    order(arrived_pair.at[0], 2, ordered_pair)
     place_chunk(0, 2, ordered_pair)
     placed = fours if ends_in_pair else fours - 1
 
     def collect(four, carry):
-        for_first(
-            four,
-            lambda message, part: receive(
-                send.at[message], arrived.at[message], message, part
-            ),
-        )
-        message, half = seat(four)
-        ordering(arrived.at[message], 4, ordered, (half,))
+        receive(send.at[four], arrived.at[four], four)
 
         @pl.when(four < placed)
         def _():
+            order(arrived.at[four], 4, ordered)
             place_chunk(2 + 4 * four, 4, ordered)
 
         @pl.when(four == placed - 1)
@@ -491,11 +459,10 @@
         return carry
 
     lax.fori_loop(0, fours, collect, 0)
-    rest = ordered
+    rest = arrived.at[fours - 1]
     if ends_in_pair:
-        receive(send_pair.at[1], arrived_pair.at[1], messages + 1)
-        ordering(arrived_pair.at[1], 2, ordered_pair)
-        rest = ordered_pair
+        receive(send_pair.at[1], arrived_pair.at[1], fours + 1)
+        rest = arrived_pair.at[1]
     rest_out = pltpu.make_async_copy(rest, last, out_sem.at[1])
     rest_out.start()
 
@@ -505,16 +472,15 @@
 
     lax.fori_loop(0, depth, sent, 0)
 
-    def gone(four, carry):
-        for_message(
-            four,
-            lambda message, part: others_wait(send.at[message], send_sem.at[message], part),
-        )
+    def gone(chunk, carry):
+        departures = send.at[chunk, pl.ds(0, CHIPS - 1)]
+        pltpu.make_async_copy(departures, departures, send_sem.at[chunk]).wait()
         return carry
 
     lax.fori_loop(0, fours, gone, 0)
     for pair in range(1 + ends_in_pair):
-        others_wait(send_pair.at[pair], send_sem.at[messages + pair])
+        departures = send_pair.at[pair, pl.ds(0, CHIPS - 1)]
+        pltpu.make_async_copy(departures, departures, send_sem.at[fours + pair]).wait()
     pltpu.make_async_copy(partial, out, out_sem.at[0]).wait()
     rest_out.wait()
 
@@ -525,8 +491,7 @@
     vmem = pl.BlockSpec(memory_space=pltpu.VMEM)
     bf16 = jnp.bfloat16
     fours = fours_of(slots)
-    messages = fours // 2 + 1
-    message = (CHIPS, 2, 4 * ROWS, B)
+    messages = (CHIPS, 4 * ROWS, B)
     pair_messages = (2, CHIPS, 4 * ROWS, B // 2)
     dma = pltpu.SemaphoreType.DMA
     return pl.pallas_call(
@@ -534,7 +499,7 @@
         name=f"exchange_{slots}",
         out_shape=[
             jax.ShapeDtypeStruct((SECTORS, ROWS, SECTORS, B), bf16),
-            jax.ShapeDtypeStruct(last_shape(last_count(slots)), bf16),
+            jax.ShapeDtypeStruct((CHIPS, 4 * ROWS, B * last_count(slots) // 4), bf16),
         ],
         in_specs=[smem] * 2 + [vmem] + [anywhere] * 3,
         out_specs=[anywhere] * 2,
@@ -545,8 +510,8 @@
             pltpu.VMEM((TERMS * RIGHT_DEV, B, B), bf16),
             pltpu.VMEM((depth, CHIPS_Z, CORES, B // (CHIPS_Z * CORES), B), bf16),
             pltpu.VMEM((CORES * depth, CHIPS_Z, B // (CHIPS_Z * CORES), B), bf16),
-            pltpu.VMEM((messages, *message), bf16),
-            pltpu.VMEM((messages, *message), bf16),
+            pltpu.VMEM((fours, *messages), bf16),
+            pltpu.VMEM((fours, *messages), bf16),
             pltpu.VMEM(pair_messages, bf16),
             pltpu.VMEM(pair_messages, bf16),
             pltpu.VMEM((SECTORS, ROWS, SECTORS, B), bf16),
@@ -557,9 +522,9 @@
             dma((depth,)),
             dma((depth,)),
             pltpu.SemaphoreType.REGULAR,
-            dma((messages + 2,)),
-            dma((messages + 2,)),
-            dma((messages + 2,)),
+            dma((fours + 2,)),
+            dma((fours + 2,)),
+            dma((fours + 2,)),
             dma((2,)),
         ],
         compiler_params=pltpu.CompilerParams(
@@ -580,36 +545,41 @@
     )
 
 
-def finish_kernel(first, count, labels, partial, last, out, held, rest, sem, rest_sem):
-    parts = held.shape[0] // 8
+def finish_kernel(
+    first, count, labels, partial, last, out, held, arrived, rest, sem, rest_sem
+):
+    step = 4
+    parts = SECTORS // step
 
     def fetch(part):
-        rows = pl.ds(part * 8, 8)
+        rows = pl.ds(part * step, step)
         return pltpu.make_async_copy(partial.at[rows], held.at[rows], sem.at[part])
 
     def store(part):
-        rows = pl.ds(part * 8, 8)
+        rows = pl.ds(part * step, step)
         return pltpu.make_async_copy(held.at[rows], out.at[rows], sem.at[part])
 
-    rest_fetch = pltpu.make_async_copy(last, rest, rest_sem)
+    rest_fetch = pltpu.make_async_copy(last, arrived, rest_sem)
     rest_fetch.start()
     for part in range(parts):
         fetch(part).start()
     label = label_of(labels, first, count)
     rest_fetch.wait()
+    order(arrived, count, rest)
 
     def add(part, carry):
-        onehot = onehot_rows(label, part * 256, (256, count * CHIPS))
+        onehot = onehot_rows(label, part * step * SECTORS, (step * SECTORS, count * CHIPS))
         fetch(part).wait()
         width = rest.shape[-1]
+        here = pl.ds(part * step, step)
         for piece in range(rest.shape[0]):
             x, lanes = piece * width // B, piece * width % B
             lanes = slice(lanes, lanes + width)
             total = jnp.dot(
                 onehot, rest[piece], preferred_element_type=jnp.float32
-            ).reshape(8, SECTORS, width)
-            total = total + held[pl.ds(part * 8, 8), x, :, lanes].astype(jnp.float32)
-            held[pl.ds(part * 8, 8), x, :, lanes] = total.astype(jnp.bfloat16)
+            ).reshape(step, SECTORS, width)
+            total = total + held[here, x, :, lanes].astype(jnp.float32)
+            held[here, x, :, lanes] = total.astype(jnp.bfloat16)
         store(part).start()
         return carry
 
@@ -630,7 +600,8 @@
         scratch_shapes=[
             pltpu.VMEM(partial.shape, partial.dtype),
             pltpu.VMEM(last.shape, last.dtype),
-            pltpu.SemaphoreType.DMA((SECTORS // 8,)),
+            pltpu.VMEM(last_shape(count), last.dtype),
+            pltpu.SemaphoreType.DMA((SECTORS // 4,)),
             pltpu.SemaphoreType.DMA,
         ],
         compiler_params=pltpu.CompilerParams(vmem_limit_bytes=VMEM_LIMIT),

time: 62.6 us -> 74.7 us (1.19)
  Pallas kernels: 61.4 us -> 73.2 us
    pallas_call x1, Pallas kernels: 54.2 us -> 64.9 us  [exchanged(): pl.pallas_call(functools.partial(exchange_kernel, depth, slots), name=f'e...]
    pallas_call x1, Pallas kernels: 4.75 us -> 5.92 us  [finished(): pl.pallas_call(functools.partial(finish_kernel, slots - count, count), na...]
where the time goes in v4:
time: 74.7 us; the launch traced here: 74.5 us
  Pallas kernels  73.2 us (98%)
  between operations  0.84 us (1%)
    pallas_call x1, Pallas kernels, exchanged(): pl.pallas_call(functools.partial(exchange_kernel, depth, slots), name=f'e...  64.9 us
    pallas_call x1, Pallas kernels, finished(): pl.pallas_call(functools.partial(finish_kernel, slots - count, count), na...  5.92 us
    pallas_call x1, Pallas kernels, tables(): pl.pallas_call(table_kernel, name='tables', out_shape=[table, table, tabl...  2.43 us

profile of v4, /device:TPU:0, one launch (start us, length us, event | category | flops | bytes accessed | tf_op | source)
XLA Modules:
  0.0 74.5 jit_solution(11158135485986761063)
XLA Ops:
  0.0 2.4 %tables.1 = (s32[16,128]{1,0:T(8,128)S(1)}, s32[16,128]{1,0:T(8,128)S(1)}, s32[16,128]{1,0:T(8,128)S(1)}, s32[1,1]{1,0:T(1,128)}) custom-call(s32[2,32]{1,0:T(2,128)} %left_target.1, s32[2,32]{1,0:T(2,128)} %right_target.1, s32[1,32]{1,0:T(1,128)} %bitcast.23, s32[1,32]{1,0:T(1,128)} %bitcast.24), custom_call_target="tpu_custom_call" | custom-call | flops 16777216 | bytes 32768 | tf_op jit(solution)/shard_map/tables/pallas_call | solution.py:117
  3.1 71.3 %conditional.1 = (bf16[32,4,32,512]{3,2,1,0:T(8,128)(2,1)}) conditional(s32[]{:T(128)} %bitcast.12, (bf16[2,4,512,512]{3,2,1,0:T(8,128)(2,1)}, bf16[2,2,512,512]{3,2,1,0:T(8,128)(2,1)}, s32[16,128]{1,0:T(8,128)S(1)}, s32[16,128]{1,0:T(8,128)S(1)}, s32[16,128]{1,0:T(8,128)S(1)}, ...), branch_computations={%region_0.0_spmd, %region_1.0_spmd, %region_2.0_spmd, %region_3.0_... | conditional | flops 9126805504 | bytes 24117256 | solution.py:623
  3.3 64.9 %exchange_16.1 = (bf16[32,4,32,512]{3,2,1,0:T(8,128)(2,1)}, bf16[64,16,256]{2,1,0:T(8,128)(2,1)}) custom-call(s32[16,128]{1,0:T(8,128)S(1)} %get-tuple-element.88.items, s32[16,128]{1,0:T(8,128)S(1)} %get-tuple-element.89.sources, s32[16,128]{1,0:T(8,128)S(1)} %get-tuple-element.87.labels, bf16[4,512,2,512]{3,2,1,0:T(2,128)(2,1)} %get-tuple-element.90.psi_hbm, ...), custom_call_target="tpu_custom_call" | custom-call | flops 6442450944 | bytes 14680064 | tf_op jit(solution)/shard_map/cond/branch_2_fun/exchange_16/pallas_call | solution.py:497
  68.2 5.9 %finish_16.1 = bf16[32,4,32,512]{3,2,1,0:T(8,128)(2,1)} custom-call(s32[16,128]{1,0:T(8,128)S(1)} %get-tuple-element.87.labels, bf16[32,4,32,512]{3,2,1,0:T(8,128)(2,1)} %get-tuple-element.93.partial, bf16[64,16,256]{2,1,0:T(8,128)(2,1)} %get-tuple-element.94.last), custom_call_target="tpu_custom_call" | custom-call | flops 536870912 | bytes 9437184 | tf_op jit(solution)/shard_map/cond/branch_2_fun/finish_16/pallas_call | solution.py:594

commit v5 on v4

--- a/solution.py
+++ b/solution.py
@@ -307,7 +307,7 @@
             device_id_type=MESH,
         )
 
-    def multiply_two(step, carry):
+    def multiply_two(step):
         ranks = (2 * step, 2 * step + 1)
         halves, rights = [], []
         for rank in ranks:
@@ -327,6 +327,7 @@
             ).astype(jnp.bfloat16)
             product[rank] = moved.reshape(CHIPS_Z, CORES, B // (CHIPS_Z * CORES), B)
 
+    def swap_two(step):
         @pl.when(step == 0)
         def _():
             pl.semaphore_wait(barrier, CHIPS)
@@ -335,9 +336,13 @@
         def _():
             pl.semaphore_wait(free_sem, 1)
 
-        for rank in ranks:
+        for rank in (2 * step, 2 * step + 1):
             pair_copy(rank).start()
             own_copy(rank).start()
+
+    def advance(step, carry):
+        pl.when(step >= 0)(lambda: swap_two(step))
+        pl.when(step + 1 < depth // 2)(lambda: multiply_two(step + 1))
         return carry
 
     def arrive(rank, carry):
@@ -379,35 +384,32 @@
 
         lax.fori_loop(0, CHIPS_Z, quarter, 0, unroll=2)
 
-    def packed(outgoing, incoming, chunk, first, count):
-        pack(outgoing, first, count)
+    def depart(outgoing, incoming, chunk):
         self_copy(outgoing, incoming, chunk).start()
         for_others(functools.partial(departing, outgoing, incoming, chunk))
 
     def stage(turn, carry):
         start = jnp.maximum(4 * turn - 2, 0)
         stop = jnp.maximum(jnp.minimum(4 * turn + 2, depth), start)
-        lax.fori_loop(start // 2, stop // 2, multiply_two, 0)
+        lax.fori_loop(jnp.where(turn == 0, -1, start // 2), stop // 2, advance, 0)
         lax.fori_loop(start, stop, arrive, 0)
 
-        @pl.when(turn == 0)
-        def _():
-            packed(send_pair.at[0], arrived_pair.at[0], fours, 0, 2)
-
-        @pl.when(turn > 0)
-        def _():
-            four = turn - 1
-            packed(send.at[four], arrived.at[four], four, 2 + 4 * four, 4)
+        four = jnp.maximum(turn - 1, 0)
+        pl.when(turn == 0)(lambda: pack(send_pair.at[0], 0, 2))
+        pl.when(turn > 0)(lambda: pack(send.at[four], 2 + 4 * four, 4))
 
         @pl.when(turn < stages - 1)
         def _():
             pl.semaphore_signal(free_sem, inc=1, device_id=partner, device_id_type=MESH)
 
+        pl.when(turn == 0)(lambda: depart(send_pair.at[0], arrived_pair.at[0], fours))
+        pl.when(turn > 0)(lambda: depart(send.at[four], arrived.at[four], four))
         return carry
 
     lax.fori_loop(0, fours + 1, stage, 0)
     if ends_in_pair:
-        packed(send_pair.at[1], arrived_pair.at[1], fours + 1, slots - 2, 2)
+        pack(send_pair.at[1], slots - 2, 2)
+        depart(send_pair.at[1], arrived_pair.at[1], fours + 1)
 
     def receive(outgoing, incoming, chunk):
         self_copy(outgoing, incoming, chunk).wait()
@@ -446,10 +448,10 @@
 
     def collect(four, carry):
         receive(send.at[four], arrived.at[four], four)
+        order(arrived.at[four], 4, ordered)
 
         @pl.when(four < placed)
         def _():
-            order(arrived.at[four], 4, ordered)
             place_chunk(2 + 4 * four, 4, ordered)
 
         @pl.when(four == placed - 1)
@@ -459,10 +461,11 @@
         return carry
 
     lax.fori_loop(0, fours, collect, 0)
-    rest = arrived.at[fours - 1]
+    rest = ordered
     if ends_in_pair:
         receive(send_pair.at[1], arrived_pair.at[1], fours + 1)
-        rest = arrived_pair.at[1]
+        order(arrived_pair.at[1], 2, ordered_pair)
+        rest = ordered_pair
     rest_out = pltpu.make_async_copy(rest, last, out_sem.at[1])
     rest_out.start()
 
@@ -499,7 +502,7 @@
         name=f"exchange_{slots}",
         out_shape=[
             jax.ShapeDtypeStruct((SECTORS, ROWS, SECTORS, B), bf16),
-            jax.ShapeDtypeStruct((CHIPS, 4 * ROWS, B * last_count(slots) // 4), bf16),
+            jax.ShapeDtypeStruct(last_shape(last_count(slots)), bf16),
         ],
         in_specs=[smem] * 2 + [vmem] + [anywhere] * 3,
         out_specs=[anywhere] * 2,
@@ -545,41 +548,36 @@
     )
 
 
-def finish_kernel(
-    first, count, labels, partial, last, out, held, arrived, rest, sem, rest_sem
-):
-    step = 4
-    parts = SECTORS // step
+def finish_kernel(first, count, labels, partial, last, out, held, rest, sem, rest_sem):
+    parts = held.shape[0] // 8
 
     def fetch(part):
-        rows = pl.ds(part * step, step)
+        rows = pl.ds(part * 8, 8)
         return pltpu.make_async_copy(partial.at[rows], held.at[rows], sem.at[part])
 
     def store(part):
-        rows = pl.ds(part * step, step)
+        rows = pl.ds(part * 8, 8)
         return pltpu.make_async_copy(held.at[rows], out.at[rows], sem.at[part])
 
-    rest_fetch = pltpu.make_async_copy(last, arrived, rest_sem)
+    rest_fetch = pltpu.make_async_copy(last, rest, rest_sem)
     rest_fetch.start()
     for part in range(parts):
         fetch(part).start()
     label = label_of(labels, first, count)
     rest_fetch.wait()
-    order(arrived, count, rest)
 
     def add(part, carry):
-        onehot = onehot_rows(label, part * step * SECTORS, (step * SECTORS, count * CHIPS))
+        onehot = onehot_rows(label, part * 256, (256, count * CHIPS))
         fetch(part).wait()
         width = rest.shape[-1]
-        here = pl.ds(part * step, step)
         for piece in range(rest.shape[0]):
             x, lanes = piece * width // B, piece * width % B
             lanes = slice(lanes, lanes + width)
             total = jnp.dot(
                 onehot, rest[piece], preferred_element_type=jnp.float32
-            ).reshape(step, SECTORS, width)
-            total = total + held[here, x, :, lanes].astype(jnp.float32)
-            held[here, x, :, lanes] = total.astype(jnp.bfloat16)
+            ).reshape(8, SECTORS, width)
+            total = total + held[pl.ds(part * 8, 8), x, :, lanes].astype(jnp.float32)
+            held[pl.ds(part * 8, 8), x, :, lanes] = total.astype(jnp.bfloat16)
         store(part).start()
         return carry
 
@@ -600,8 +598,7 @@
         scratch_shapes=[
             pltpu.VMEM(partial.shape, partial.dtype),
             pltpu.VMEM(last.shape, last.dtype),
-            pltpu.VMEM(last_shape(count), last.dtype),
-            pltpu.SemaphoreType.DMA((SECTORS // 4,)),
+            pltpu.SemaphoreType.DMA((SECTORS // 8,)),
             pltpu.SemaphoreType.DMA,
         ],
         compiler_params=pltpu.CompilerParams(vmem_limit_bytes=VMEM_LIMIT),

time: 74.7 us -> 73.9 us (0.989)
    pallas_call x1, Pallas kernels: 5.92 us -> 4.75 us  [finished(): pl.pallas_call(functools.partial(finish_kernel, slots - count, count), na...]
where the time goes in v5:
time: 73.9 us; the launch traced here: 73.8 us
  Pallas kernels  72.5 us (98%)
  between operations  0.84 us (1%)
    pallas_call x1, Pallas kernels, exchanged(): pl.pallas_call(functools.partial(exchange_kernel, depth, slots), name=f'e...  65.4 us
    pallas_call x1, Pallas kernels, finished(): pl.pallas_call(functools.partial(finish_kernel, slots - count, count), na...  4.75 us
    pallas_call x1, Pallas kernels, tables(): pl.pallas_call(table_kernel, name='tables', out_shape=[table, table, tabl...  2.43 us

profile of v5, /device:TPU:0, one launch (start us, length us, event | category | flops | bytes accessed | tf_op | source)
XLA Modules:
  0.0 73.8 jit_solution(17868795858101519339)
XLA Ops:
  0.0 2.4 %tables.1 = (s32[16,128]{1,0:T(8,128)S(1)}, s32[16,128]{1,0:T(8,128)S(1)}, s32[16,128]{1,0:T(8,128)S(1)}, s32[1,1]{1,0:T(1,128)}) custom-call(s32[2,32]{1,0:T(2,128)} %left_target.1, s32[2,32]{1,0:T(2,128)} %right_target.1, s32[1,32]{1,0:T(1,128)} %bitcast.23, s32[1,32]{1,0:T(1,128)} %bitcast.24), custom_call_target="tpu_custom_call" | custom-call | flops 16777216 | bytes 32768 | tf_op jit(solution)/shard_map/tables/pallas_call | solution.py:117
  3.1 70.5 %conditional.1 = (bf16[32,4,32,512]{3,2,1,0:T(8,128)(2,1)}) conditional(s32[]{:T(128)} %bitcast.12, (bf16[2,4,512,512]{3,2,1,0:T(8,128)(2,1)}, bf16[2,2,512,512]{3,2,1,0:T(8,128)(2,1)}, s32[16,128]{1,0:T(8,128)S(1)}, s32[16,128]{1,0:T(8,128)S(1)}, s32[16,128]{1,0:T(8,128)S(1)}, ...), branch_computations={%region_0.0_spmd, %region_1.0_spmd, %region_2.0_spmd, %region_3.0_... | conditional | flops 9126805504 | bytes 24117256 | solution.py:620
  3.3 65.4 %exchange_16.1 = (bf16[32,4,32,512]{3,2,1,0:T(8,128)(2,1)}, bf16[8,128,256]{2,1,0:T(8,128)(2,1)}) custom-call(s32[16,128]{1,0:T(8,128)S(1)} %get-tuple-element.88.items, s32[16,128]{1,0:T(8,128)S(1)} %get-tuple-element.89.sources, s32[16,128]{1,0:T(8,128)S(1)} %get-tuple-element.87.labels, bf16[4,512,2,512]{3,2,1,0:T(2,128)(2,1)} %get-tuple-element.90.psi_hbm, ...), custom_call_target="tpu_custom_call" | custom-call | flops 6442450944 | bytes 14680064 | tf_op jit(solution)/shard_map/cond/branch_2_fun/exchange_16/pallas_call | solution.py:500
  68.7 4.7 %finish_16.1 = bf16[32,4,32,512]{3,2,1,0:T(8,128)(2,1)} custom-call(s32[16,128]{1,0:T(8,128)S(1)} %get-tuple-element.87.labels, bf16[32,4,32,512]{3,2,1,0:T(8,128)(2,1)} %get-tuple-element.93.partial, bf16[8,128,256]{2,1,0:T(8,128)(2,1)} %get-tuple-element.94.last), custom_call_target="tpu_custom_call" | custom-call | flops 536870912 | bytes 9437184 | tf_op jit(solution)/shard_map/cond/branch_2_fun/finish_16/pallas_call | solution.py:592

commit v6 on v5

--- a/solution.py
+++ b/solution.py
@@ -231,7 +231,7 @@
     ]
     left_load = pltpu.make_async_copy(left_hbm, left, in_sem.at[LEFT_DEV])
     right_load = pltpu.make_async_copy(right_hbm, right, in_sem.at[LEFT_DEV + 1])
-    for load in psi_load:
+    for load in (*psi_load, left_load, right_load):
         load.start()
 
     steps = (1, 3, 2, 0)
@@ -280,8 +280,6 @@
         return carry
 
     psi_load[0].wait()
-    left_load.start()
-    right_load.start()
     split(0, 0)
 
     def next_split(a, carry):
@@ -560,7 +558,7 @@
         return pltpu.make_async_copy(held.at[rows], out.at[rows], sem.at[part])
 
     rest_fetch = pltpu.make_async_copy(last, rest, rest_sem)
-    rest_fetch.start()
+    rest_fetch.start(priority=1)
     for part in range(parts):
         fetch(part).start()
     label = label_of(labels, first, count)

time: 73.9 us -> 62.6 us (0.85)
  Pallas kernels: 72.5 us -> 61.3 us
    pallas_call x1, Pallas kernels: 65.4 us -> 53.8 us  [exchanged(): pl.pallas_call(functools.partial(exchange_kernel, depth, slots), name=f'e...]
where the time goes in v6:
time: 62.6 us; the launch traced here: 62.4 us
  Pallas kernels  61.3 us (98%)
  between operations  0.84 us (1%)
    pallas_call x1, Pallas kernels, exchanged(): pl.pallas_call(functools.partial(exchange_kernel, depth, slots), name=f'e...  53.8 us
    pallas_call x1, Pallas kernels, finished(): pl.pallas_call(functools.partial(finish_kernel, slots - count, count), na...  5.07 us
    pallas_call x1, Pallas kernels, tables(): pl.pallas_call(table_kernel, name='tables', out_shape=[table, table, tabl...  2.43 us

profile of v6, /device:TPU:0, one launch (start us, length us, event | category | flops | bytes accessed | tf_op | source)
XLA Modules:
  0.0 62.4 jit_solution(1797063227619923442)
XLA Ops:
  0.0 2.4 %tables.1 = (s32[16,128]{1,0:T(8,128)S(1)}, s32[16,128]{1,0:T(8,128)S(1)}, s32[16,128]{1,0:T(8,128)S(1)}, s32[1,1]{1,0:T(1,128)}) custom-call(s32[2,32]{1,0:T(2,128)} %left_target.1, s32[2,32]{1,0:T(2,128)} %right_target.1, s32[1,32]{1,0:T(1,128)} %bitcast.23, s32[1,32]{1,0:T(1,128)} %bitcast.24), custom_call_target="tpu_custom_call" | custom-call | flops 16777216 | bytes 32768 | tf_op jit(solution)/shard_map/tables/pallas_call | solution.py:117
  3.1 59.2 %conditional.1 = (bf16[32,4,32,512]{3,2,1,0:T(8,128)(2,1)}) conditional(s32[]{:T(128)} %bitcast.12, (bf16[2,4,512,512]{3,2,1,0:T(8,128)(2,1)}, bf16[2,2,512,512]{3,2,1,0:T(8,128)(2,1)}, s32[16,128]{1,0:T(8,128)S(1)}, s32[16,128]{1,0:T(8,128)S(1)}, s32[16,128]{1,0:T(8,128)S(1)}, ...), branch_computations={%region_0.0_spmd, %region_1.0_spmd, %region_2.0_spmd, %region_3.0_... | conditional | flops 9126805504 | bytes 24117256 | solution.py:618
  3.1 53.8 %exchange_12.1 = (bf16[32,4,32,512]{3,2,1,0:T(8,128)(2,1)}, bf16[8,128,256]{2,1,0:T(8,128)(2,1)}) custom-call(s32[16,128]{1,0:T(8,128)S(1)} %get-tuple-element.70.items, s32[16,128]{1,0:T(8,128)S(1)} %get-tuple-element.72.sources, s32[16,128]{1,0:T(8,128)S(1)} %get-tuple-element.62.labels, bf16[4,512,2,512]{3,2,1,0:T(2,128)(2,1)} %get-tuple-element.74.psi_hbm, ...), custom_call_target="tpu_custom_call" | custom-call | flops 5368709120 | bytes 14680064 | tf_op jit(solution)/shard_map/cond/branch_0_fun/exchange_12/pallas_call | solution.py:498
  57.0 5.1 %finish_12.1 = bf16[32,4,32,512]{3,2,1,0:T(8,128)(2,1)} custom-call(s32[16,128]{1,0:T(8,128)S(1)} %get-tuple-element.62.labels, bf16[32,4,32,512]{3,2,1,0:T(8,128)(2,1)} %get-tuple-element.77.partial, bf16[8,128,256]{2,1,0:T(8,128)(2,1)} %get-tuple-element.78.last), custom_call_target="tpu_custom_call" | custom-call | flops 536870912 | bytes 9437184 | tf_op jit(solution)/shard_map/cond/branch_0_fun/finish_12/pallas_call | solution.py:590

commit v7 on v6

--- a/solution.py
+++ b/solution.py
@@ -195,6 +195,7 @@
     left,
     right,
     product,
+    both_first,
     both,
     send,
     arrived,
@@ -221,7 +222,6 @@
     here = z * RIGHT + place
     device = (z * CORES + core) * RIGHT + place
     fours = fours_of(slots)
-    stages = -(-(depth + 2) // 4)
     ends_in_pair = last_count(slots) == 2
 
     psi_rows = psi_hbm.reshape(LEFT_DEV, B * RIGHT_DEV, B)
@@ -290,22 +290,27 @@
     left_load.wait()
     right_load.wait()
 
-    def own_copy(rank):
+    def half_of(rank, first):
+        if first:
+            return both_first.at[core * 2 + rank]
+        return both.at[core * (depth - 2) + rank - 2]
+
+    def own_copy(rank, first):
         return pltpu.make_async_copy(
-            product.at[rank, :, core], both.at[core * depth + rank], own_sem.at[rank]
+            product.at[rank, :, core], half_of(rank, first), own_sem.at[rank]
         )
 
-    def pair_copy(rank):
+    def pair_copy(rank, first):
         return pltpu.make_async_remote_copy(
             src_ref=product.at[rank, :, other],
-            dst_ref=both.at[core * depth + rank],
+            dst_ref=half_of(rank, first),
             send_sem=pair_send_sem.at[rank],
             recv_sem=pair_recv_sem.at[rank],
             device_id=partner,
             device_id_type=MESH,
         )
 
-    def multiply_two(step):
+    def multiply_two(step, carry):
         ranks = (2 * step, 2 * step + 1)
         halves, rights = [], []
         for rank in ranks:
@@ -325,28 +330,22 @@
             ).astype(jnp.bfloat16)
             product[rank] = moved.reshape(CHIPS_Z, CORES, B // (CHIPS_Z * CORES), B)
 
-    def swap_two(step):
-        @pl.when(step == 0)
-        def _():
-            pl.semaphore_wait(barrier, CHIPS)
-
-        @pl.when((step > 0) & (step % 2 == 1))
-        def _():
-            pl.semaphore_wait(free_sem, 1)
-
-        for rank in (2 * step, 2 * step + 1):
-            pair_copy(rank).start()
-            own_copy(rank).start()
-
-    def advance(step, carry):
-        pl.when(step >= 0)(lambda: swap_two(step))
-        pl.when(step + 1 < depth // 2)(lambda: multiply_two(step + 1))
         return carry
 
-    def arrive(rank, carry):
-        own_copy(rank).wait()
-        pair_copy(rank).wait_recv()
-        return carry
+    def swap(rank, first):
+        pair_copy(rank, first).start()
+        own_copy(rank, first).start()
+
+    def arrive(rank, first):
+        own_copy(rank, first).wait()
+        pair_copy(rank, first).wait_recv()
+
+    def for_ranks(start, stop, visit):
+        def one(rank, carry):
+            visit(rank, False)
+            return carry
+
+        lax.fori_loop(start, stop, one, 0)
 
     def departing(outgoing, incoming, chunk, far_z, far_place):
         pltpu.make_async_remote_copy(
@@ -365,11 +364,16 @@
 
     mix = exchange(4, 64)
 
-    def pack(outgoing, first, count):
+    def pack(outgoing, first, count, early=False):
         def quarter(far_z, carry):
             def block(k):
                 source = sources[first // 2 + k // 2, k % 2 * CHIPS + here]
-                return both[source // ITEMS * depth + source % ITEMS, far_z]
+                of_core, rank = source // ITEMS, source % ITEMS
+                rows = both_first[of_core * 2 + jnp.minimum(rank, 1), far_z]
+                if early:
+                    return rows
+                later = both[of_core * (depth - 2) + jnp.maximum(rank - 2, 0), far_z]
+                return jnp.where(rank < 2, rows, later)
 
             blocks = [block(k) for k in range(count)]
             if count == 2:
@@ -386,22 +390,39 @@
         self_copy(outgoing, incoming, chunk).start()
         for_others(functools.partial(departing, outgoing, incoming, chunk))
 
+    steps_all = depth // 2
+
     def stage(turn, carry):
-        start = jnp.maximum(4 * turn - 2, 0)
-        stop = jnp.maximum(jnp.minimum(4 * turn + 2, depth), start)
-        lax.fori_loop(jnp.where(turn == 0, -1, start // 2), stop // 2, advance, 0)
-        lax.fori_loop(start, stop, arrive, 0)
-
+        start = jnp.where(turn == 0, 0, jnp.minimum(2 * turn + 1, steps_all))
+        stop = jnp.minimum(2 * turn + 3, steps_all)
+        lax.fori_loop(start, stop, multiply_two, 0)
         four = jnp.maximum(turn - 1, 0)
-        pl.when(turn == 0)(lambda: pack(send_pair.at[0], 0, 2))
-        pl.when(turn > 0)(lambda: pack(send.at[four], 2 + 4 * four, 4))
-
-        @pl.when(turn < stages - 1)
+
+        @pl.when(turn == 0)
         def _():
-            pl.semaphore_signal(free_sem, inc=1, device_id=partner, device_id_type=MESH)
-
-        pl.when(turn == 0)(lambda: depart(send_pair.at[0], arrived_pair.at[0], fours))
-        pl.when(turn > 0)(lambda: depart(send.at[four], arrived.at[four], four))
+            pl.semaphore_wait(barrier, CHIPS)
+            for rank in range(2):
+                swap(rank, True)
+            for_ranks(2, 6, swap)
+            for rank in range(2):
+                arrive(rank, True)
+            pack(send_pair.at[0], 0, 2, early=True)
+            depart(send_pair.at[0], arrived_pair.at[0], fours)
+
+        @pl.when(turn > 0)
+        def _():
+            here_from = jnp.minimum(4 * turn - 2, depth)
+            for_ranks(here_from, jnp.minimum(4 * turn + 2, depth), arrive)
+            pack(send.at[four], 2 + 4 * four, 4)
+
+            @pl.when(start < stop)
+            def _():
+                pl.semaphore_signal(free_sem, inc=1, device_id=partner, device_id_type=MESH)
+                pl.semaphore_wait(free_sem, 1)
+                for_ranks(2 * start, 2 * stop, swap)
+
+            depart(send.at[four], arrived.at[four], four)
+
         return carry
 
     lax.fori_loop(0, fours + 1, stage, 0)
@@ -467,11 +488,9 @@
     rest_out = pltpu.make_async_copy(rest, last, out_sem.at[1])
     rest_out.start()
 
-    def sent(rank, carry):
-        pair_copy(rank).wait_send()
-        return carry
-
-    lax.fori_loop(0, depth, sent, 0)
+    for rank in range(2):
+        pair_copy(rank, True).wait_send()
+    for_ranks(2, depth, lambda rank, first: pair_copy(rank, first).wait_send())
 
     def gone(chunk, carry):
         departures = send.at[chunk, pl.ds(0, CHIPS - 1)]
@@ -510,7 +529,8 @@
             pltpu.VMEM((TERMS * LEFT_DEV, B, B), bf16),
             pltpu.VMEM((TERMS * RIGHT_DEV, B, B), bf16),
             pltpu.VMEM((depth, CHIPS_Z, CORES, B // (CHIPS_Z * CORES), B), bf16),
-            pltpu.VMEM((CORES * depth, CHIPS_Z, B // (CHIPS_Z * CORES), B), bf16),
+            pltpu.VMEM((CORES * 2, CHIPS_Z, B // (CHIPS_Z * CORES), B), bf16),
+            pltpu.VMEM((CORES * (depth - 2), CHIPS_Z, B // (CHIPS_Z * CORES), B), bf16),
             pltpu.VMEM((fours, *messages), bf16),
             pltpu.VMEM((fours, *messages), bf16),
             pltpu.VMEM(pair_messages, bf16),
@@ -558,7 +578,7 @@
         return pltpu.make_async_copy(held.at[rows], out.at[rows], sem.at[part])
 
     rest_fetch = pltpu.make_async_copy(last, rest, rest_sem)
-    rest_fetch.start(priority=1)
+    rest_fetch.start()
     for part in range(parts):
         fetch(part).start()
     label = label_of(labels, first, count)

time: 62.6 us -> 82 us (1.31)
  Pallas kernels: 61.3 us -> 80.6 us
    pallas_call x1, Pallas kernels: 53.8 us -> 73.1 us  [exchanged(): pl.pallas_call(functools.partial(exchange_kernel, depth, slots), name=f'e...]
where the time goes in v7:
time: 82 us; the launch traced here: 81.9 us
  Pallas kernels  80.6 us (98%)
  between operations  0.84 us (1%)
    pallas_call x1, Pallas kernels, exchanged(): pl.pallas_call(functools.partial(exchange_kernel, depth, slots), name=f'e...  73.1 us
    pallas_call x1, Pallas kernels, finished(): pl.pallas_call(functools.partial(finish_kernel, slots - count, count), na...  5.01 us
    pallas_call x1, Pallas kernels, tables(): pl.pallas_call(table_kernel, name='tables', out_shape=[table, table, tabl...  2.43 us

profile of v7, /device:TPU:0, one launch (start us, length us, event | category | flops | bytes accessed | tf_op | source)
XLA Modules:
  0.0 81.9 jit_solution(5852343022601518964)
XLA Ops:
  0.0 2.4 %tables.1 = (s32[16,128]{1,0:T(8,128)S(1)}, s32[16,128]{1,0:T(8,128)S(1)}, s32[16,128]{1,0:T(8,128)S(1)}, s32[1,1]{1,0:T(1,128)}) custom-call(s32[2,32]{1,0:T(2,128)} %left_target.1, s32[2,32]{1,0:T(2,128)} %right_target.1, s32[1,32]{1,0:T(1,128)} %bitcast.23, s32[1,32]{1,0:T(1,128)} %bitcast.24), custom_call_target="tpu_custom_call" | custom-call | flops 16777216 | bytes 32768 | tf_op jit(solution)/shard_map/tables/pallas_call | solution.py:117
  3.1 78.6 %conditional.1 = (bf16[32,4,32,512]{3,2,1,0:T(8,128)(2,1)}) conditional(s32[]{:T(128)} %bitcast.12, (bf16[2,4,512,512]{3,2,1,0:T(8,128)(2,1)}, bf16[2,2,512,512]{3,2,1,0:T(8,128)(2,1)}, s32[16,128]{1,0:T(8,128)S(1)}, s32[16,128]{1,0:T(8,128)S(1)}, s32[16,128]{1,0:T(8,128)S(1)}, ...), branch_computations={%region_0.0_spmd, %region_1.0_spmd, %region_2.0_spmd, %region_3.0_... | conditional | flops 9126805504 | bytes 24117256 | solution.py:638
  3.3 73.1 %exchange_18.1 = (bf16[32,4,32,512]{3,2,1,0:T(8,128)(2,1)}, bf16[4,256,512]{2,1,0:T(8,128)(2,1)}) custom-call(s32[16,128]{1,0:T(8,128)S(1)} %get-tuple-element.96.items, s32[16,128]{1,0:T(8,128)S(1)} %get-tuple-element.97.sources, s32[16,128]{1,0:T(8,128)S(1)} %get-tuple-element.95.labels, bf16[4,512,2,512]{3,2,1,0:T(2,128)(2,1)} %get-tuple-element.98.psi_hbm, ...), custom_call_target="tpu_custom_call" | custom-call | flops 6442450944 | bytes 14680064 | tf_op jit(solution)/shard_map/cond/branch_3_fun/exchange_18/pallas_call | solution.py:517
  76.4 5.0 %finish_18.1 = bf16[32,4,32,512]{3,2,1,0:T(8,128)(2,1)} custom-call(s32[16,128]{1,0:T(8,128)S(1)} %get-tuple-element.95.labels, bf16[32,4,32,512]{3,2,1,0:T(8,128)(2,1)} %get-tuple-element.101.partial, bf16[4,256,512]{2,1,0:T(8,128)(2,1)} %get-tuple-element.102.last), custom_call_target="tpu_custom_call" | custom-call | flops 1073741824 | bytes 9437184 | tf_op jit(solution)/shard_map/cond/branch_3_fun/finish_18/pallas_call | solution.py:610

commit v8 on v6

--- a/solution.py
+++ b/solution.py
@@ -266,27 +266,37 @@
             barrier, inc=1, device_id=(far_z, core, far_place), device_id_type=MESH
         )
 
-    for_others(greet)
+    def greet_turn(shift):
+        far_z = [
+            (z + 2 * CHIPS_Z + way * (shift + step)) % CHIPS_Z for step in range(CHIPS_Z)
+        ]
+        for moved, step, far_place in route:
+            if moved or step:
+                greet(far_z[step], far_place)
+
+    for step in range(1, CHIPS_Z):
+        greet((z + step) % CHIPS_Z, place)
+    greet_turn(0)
 
     unmix = exchange(128, RIGHT_DEV)
 
-    def split(a, carry):
+    def split(a):
         for part in range(B // 128):
             apart = reorder(unmix, landed[a, part * 256 : part * 256 + 256, :])
             for b in range(RIGHT_DEV):
                 psi[a * RIGHT_DEV + b, part * 128 : part * 128 + 128, :] = apart[
                     b * 128 : (b + 1) * 128
                 ]
-        return carry
-
-    psi_load[0].wait()
-    split(0, 0)
-
-    def next_split(a, carry):
+
+    def greet_and_split(a, carry):
         pltpu.make_async_copy(psi_rows.at[a], landed.at[a], in_sem.at[a]).wait()
-        return split(a, carry)
-
-    lax.fori_loop(1, LEFT_DEV, next_split, 0)
+        greet_turn(a + 1)
+        split(a)
+        return carry
+
+    lax.fori_loop(0, LEFT_DEV - 1, greet_and_split, 0)
+    psi_load[LEFT_DEV - 1].wait()
+    split(LEFT_DEV - 1)
     left_load.wait()
     right_load.wait()
 
@@ -558,7 +568,7 @@
         return pltpu.make_async_copy(held.at[rows], out.at[rows], sem.at[part])
 
     rest_fetch = pltpu.make_async_copy(last, rest, rest_sem)
-    rest_fetch.start(priority=1)
+    rest_fetch.start()
     for part in range(parts):
         fetch(part).start()
     label = label_of(labels, first, count)

time: 62.6 us -> 68.1 us (1.088)
  Pallas kernels: 61.3 us -> 66.9 us
    pallas_call x1, Pallas kernels: 53.8 us -> 59.4 us  [exchanged(): pl.pallas_call(functools.partial(exchange_kernel, depth, slots), name=f'e...]
where the time goes in v8:
time: 68.1 us; the launch traced here: 68 us
  Pallas kernels  66.9 us (98%)
  between operations  0.84 us (1%)
    pallas_call x1, Pallas kernels, exchanged(): pl.pallas_call(functools.partial(exchange_kernel, depth, slots), name=f'e...  59.4 us
    pallas_call x1, Pallas kernels, finished(): pl.pallas_call(functools.partial(finish_kernel, slots - count, count), na...  5.01 us
    pallas_call x1, Pallas kernels, tables(): pl.pallas_call(table_kernel, name='tables', out_shape=[table, table, tabl...  2.43 us

profile of v8, /device:TPU:0, one launch (start us, length us, event | category | flops | bytes accessed | tf_op | source)
XLA Modules:
  0.0 68.0 jit_solution(5095285345101270984)
XLA Ops:
  0.0 2.4 %tables.1 = (s32[16,128]{1,0:T(8,128)S(1)}, s32[16,128]{1,0:T(8,128)S(1)}, s32[16,128]{1,0:T(8,128)S(1)}, s32[1,1]{1,0:T(1,128)}) custom-call(s32[2,32]{1,0:T(2,128)} %left_target.1, s32[2,32]{1,0:T(2,128)} %right_target.1, s32[1,32]{1,0:T(1,128)} %bitcast.23, s32[1,32]{1,0:T(1,128)} %bitcast.24), custom_call_target="tpu_custom_call" | custom-call | flops 16777216 | bytes 32768 | tf_op jit(solution)/shard_map/tables/pallas_call | solution.py:117
  3.1 64.7 %conditional.1 = (bf16[32,4,32,512]{3,2,1,0:T(8,128)(2,1)}) conditional(s32[]{:T(128)} %bitcast.12, (bf16[2,4,512,512]{3,2,1,0:T(8,128)(2,1)}, bf16[2,2,512,512]{3,2,1,0:T(8,128)(2,1)}, s32[16,128]{1,0:T(8,128)S(1)}, s32[16,128]{1,0:T(8,128)S(1)}, s32[16,128]{1,0:T(8,128)S(1)}, ...), branch_computations={%region_0.0_spmd, %region_1.0_spmd, %region_2.0_spmd, %region_3.0_... | conditional | flops 9126805504 | bytes 24117256 | solution.py:628
  3.1 59.4 %exchange_14.1 = (bf16[32,4,32,512]{3,2,1,0:T(8,128)(2,1)}, bf16[4,256,512]{2,1,0:T(8,128)(2,1)}) custom-call(s32[16,128]{1,0:T(8,128)S(1)} %get-tuple-element.80.items, s32[16,128]{1,0:T(8,128)S(1)} %get-tuple-element.81.sources, s32[16,128]{1,0:T(8,128)S(1)} %get-tuple-element.79.labels, bf16[4,512,2,512]{3,2,1,0:T(2,128)(2,1)} %get-tuple-element.82.psi_hbm, ...), custom_call_target="tpu_custom_call" | custom-call | flops 5368709120 | bytes 14680064 | tf_op jit(solution)/shard_map/cond/branch_1_fun/exchange_14/pallas_call | solution.py:508
  62.5 5.0 %finish_14.1 = bf16[32,4,32,512]{3,2,1,0:T(8,128)(2,1)} custom-call(s32[16,128]{1,0:T(8,128)S(1)} %get-tuple-element.79.labels, bf16[32,4,32,512]{3,2,1,0:T(8,128)(2,1)} %get-tuple-element.85.partial, bf16[4,256,512]{2,1,0:T(8,128)(2,1)} %get-tuple-element.86.last), custom_call_target="tpu_custom_call" | custom-call | flops 1073741824 | bytes 9437184 | tf_op jit(solution)/shard_map/cond/branch_1_fun/finish_14/pallas_call | solution.py:600
